TPU v7x, 256 devices: a whole 4x4x8 slice. The times are simulated.
256 devices in a mesh: aux: 8 (over z), tile: 32 (over y, x, core).
Axes of the slice: x: 4, y: 4, z: 8, core: 2. Of those that a mesh axis runs over, the one named last changes fastest.
Arguments:
- transformed: bfloat16 [4096, 106496], P('aux', 'tile'), may hold values from -6 to 6
- coupling: bfloat16 [4096, 4096], P('aux'), may hold values from -0.09375 to 0.09375
- block_mask: int32 [32, 32], replicated, may hold values 0 or 1
- density_row: bfloat16 [16384, 128], P('tile'), may hold values from -0.5 to 0.5
- density_col: bfloat16 [16384, 128], P('tile'), may hold values from -0.5 to 0.5
- row_owner: int32 [832, 1], replicated, may hold values from 0 to 31; in each aligned block of 26 rows (0 to 25, 26 to 51, ...) at most 2 rows name the same one
- row_slot: int32 [832, 1], replicated, may hold values from 0 to 3
- col_owner: int32 [832, 1], replicated, may hold values from 0 to 31; in each aligned block of 26 rows (0 to 25, 26 to 51, ...) at most 2 rows name the same one
- col_slot: int32 [832, 1], replicated, may hold values from 0 to 3
Outputs:
- grad_row: float32 [4096, 16384], P('aux', 'tile')
- grad_col: float32 [4096, 16384], P('aux', 'tile')
Inputs may be any that keep to these rules, and one draw needn't show every extreme that they name: `row_owner`: among the 26 tiles of one index of tile (aligned blocks of rows), no owner is named more than 2 times, a bound that some block reaches. `col_owner`: as for row_owner.
All inputs are finite; a program needn't handle non-finite values.
Results may differ from a plain program's by a relative error of at most 0.0041.
Values may be sent and summed in bfloat16 or wider, within the bound.
A program may use at most 128 MiB of HBM per device.

v0:
```python
import jax
import jax.numpy as jnp
from jax import lax
from jax.sharding import PartitionSpec as P


def shards(
    transformed,
    coupling,
    block_mask,
    density_row,
    density_col,
    row_owner,
    row_slot,
    col_owner,
    col_slot,
):
    aux_dev = coupling.shape[0]
    naux = coupling.shape[1]
    zblock = naux // block_mask.shape[0]
    n_tile = lax.axis_size("tile")
    me_aux = lax.axis_index("aux")
    me_tile = lax.axis_index("tile")
    mask_rows = lax.dynamic_slice_in_dim(
        block_mask, me_aux * (aux_dev // zblock), aux_dev // zblock, 0
    )
    expanded = jnp.repeat(jnp.repeat(mask_rows, zblock, axis=0), zblock, axis=1).astype(
        jnp.bfloat16
    )
    masked = coupling * expanded
    pairs = transformed.shape[1]
    summed = jnp.dot(
        masked,
        lax.all_gather(transformed, "aux", axis=0, tiled=True),
        preferred_element_type=jnp.float32,
    )
    gtiles = summed.astype(jnp.bfloat16)
    width = density_row.shape[1]
    tiles_dev = pairs // width
    blk_dev = density_row.shape[0] // width
    capacity = max(2, 2 * tiles_dev // n_tile)
    three = gtiles.reshape(aux_dev, tiles_dev, width)
    first = me_tile * tiles_dev

    def pack(owner_list, slot_list):
        owners = lax.dynamic_slice_in_dim(owner_list[:, 0], first, tiles_dev, 0)
        slots = lax.dynamic_slice_in_dim(slot_list[:, 0], first, tiles_dev, 0)
        dest_hot = (owners[:, None] == jnp.arange(n_tile, dtype=jnp.int32)[None, :]).astype(
            jnp.int32
        )
        rank = jnp.sum(jnp.cumsum(dest_hot, axis=0) * dest_hot, axis=1) - 1
        target = owners * capacity + rank
        place = (target[None, :] == jnp.arange(n_tile * capacity, dtype=jnp.int32)[:, None]).astype(
            jnp.bfloat16
        )
        packed = jnp.einsum("st,ptk->spk", place, three, preferred_element_type=jnp.float32).astype(
            jnp.bfloat16
        )
        slot_hot = (slots[:, None] == jnp.arange(blk_dev, dtype=jnp.int32)[None, :]).astype(
            jnp.bfloat16
        )
        marks = jnp.dot(place, slot_hot, preferred_element_type=jnp.float32).astype(jnp.bfloat16)
        return (
            packed.reshape(n_tile, capacity, aux_dev, width),
            marks.reshape(n_tile, capacity, blk_dev),
        )

    send_row, mark_row = pack(row_owner, row_slot)
    send_col, mark_col = pack(col_owner, col_slot)
    recv_row, got_row, recv_col, got_col = (
        lax.all_to_all(send_row, "tile", split_axis=0, concat_axis=0, tiled=True),
        lax.all_to_all(mark_row, "tile", split_axis=0, concat_axis=0, tiled=True),
        lax.all_to_all(send_col, "tile", split_axis=0, concat_axis=0, tiled=True),
        lax.all_to_all(mark_col, "tile", split_axis=0, concat_axis=0, tiled=True),
    )

    def contract(received, marks, density):
        flat = received.reshape(n_tile * capacity, aux_dev, width)
        weights = marks.reshape(n_tile * capacity, blk_dev)
        totals = jnp.einsum(
            "sb,spk->bpk", weights, flat, preferred_element_type=jnp.float32
        ).astype(jnp.bfloat16)
        dens = density.reshape(blk_dev, width, width)
        result = jnp.einsum("bph,bhk->pbk", totals, dens, preferred_element_type=jnp.float32)
        return result.reshape(aux_dev, blk_dev * width)

    grad_row = contract(recv_row, got_row, density_row)
    grad_col = contract(recv_col, got_col, density_col)
    return (grad_row, grad_col)


def solution(mesh):
    placed = (
        P("aux", "tile"),
        P("aux", None),
        P(),
        P("tile", None),
        P("tile", None),
        P(),
        P(),
        P(),
        P(),
    )
    return jax.shard_map(
        shards,
        mesh=mesh,
        in_specs=placed,
        out_specs=(P("aux", "tile"), P("aux", "tile")),
        check_vma=False,
    )
```

profile of v0, /device:TPU:2, one launch (start us, length us, event | category | flops | bytes accessed | tf_op | source)
XLA Modules:
  0.0 576.4 jit_solution(12720364471409814906)
XLA Ops:
  7.2 0.7 all-gather.2.cloned.1.call-update
  7.9 0.8 fusion.35
  8.8 0.8 fusion.37
  9.6 0.2 select_reduce_fusion.1
  9.8 0.3 convolution_convert_fusion.4
  10.0 0.7 copy.41
  10.8 7.6 %all-to-all-start = ((bf16[32,2,4]{2,1,0:T(2,128)(2,1)}), bf16[32,2,4]{2,1,0:T(2,128)(2,1)S(1)}, u32[]{:S(2)}, u32[]{:S(2)}) async-start(bf16[32,2,4]{2,1,0:T(2,128)(2,1)} %bitcast.2), calls=%async_computation | async-start | bytes 32768 | tf_op jit(solution)/shard_map/all_to_all | solution.py:72
  18.5 0.2 select_reduce_fusion
  18.7 0.3 convolution_convert_fusion.3
  19.0 0.7 copy.49
  19.7 0.7 dynamic-slice_convert_fusion
  20.4 263.5 %all-gather.2.cloned.1.call-done = bf16[4096,3328]{1,0:T(8,128)(2,1)} async-done(((bf16[512,3328]{1,0:T(8,128)(2,1)}), bf16[4096,3328]{1,0:T(8,128)(2,1)}) %all-gather.2.cloned.1.call-update) | async-done | bytes 27262992 | tf_op jit(solution)/shard_map/all_gather | solution.py:34
  283.9 3.7 broadcast_in_dim.5
  287.6 24.6 %convolution_convert_fusion.2 = bf16[512,3328]{1,0:T(8,128)(2,1)} fusion(bf16[4096,3328]{1,0:T(8,128)(2,1)} %all-gather.2.cloned.1.call-done, bf16[512,4096]{1,0:T(8,128)(2,1)} %param.10, bf16[64,8,32,128]{3,2,1,0:T(8,128)(2,1)S(1)} %bitcast.57), kind=kOutput, calls=%fused_computation.6 | convolution fusion | flops 13962444800 | bytes 39059456 | tf_op jit(solution)/shard_map/dot_general | solution.py:32
  312.2 4.2 copy.42
  316.4 6.3 %copy.43 = bf16[512,26,128]{2,1,0:T(8,128)(2,1)} copy(bf16[512,26,128]{0,2,1:T(8,128)(2,1)S(1)} %bitcast.56) | data formatting | bytes 6815744 | tf_op jit(solution)/shard_map/reshape | solution.py:42
  322.7 7.4 %all-to-all-start.2 = ((bf16[32,2,4]{2,1,0:T(2,128)(2,1)}), bf16[32,2,4]{2,1,0:T(2,128)(2,1)S(1)}, u32[]{:S(2)}, u32[]{:S(2)}) async-start(bf16[32,2,4]{2,1,0:T(2,128)(2,1)} %bitcast.62), calls=%async_computation.2 | async-start | bytes 32768 | tf_op jit(solution)/shard_map/all_to_all | solution.py:74
  330.2 4.6 convolution_convert_fusion.1
  334.8 7.0 %copy.44 = bf16[32,2,512,128]{3,1,2,0:T(2,128)(2,1)} copy(bf16[32,2,512,128]{3,1,0,2:T(2,128)(2,1)S(1)} %bitcast.55) | data formatting | bytes 16777216 | tf_op jit(solution)/shard_map/reshape | solution.py:64
  341.9 7.4 %all-to-all-start.1 = ((bf16[32,2,512,128]{3,1,2,0:T(2,128)(2,1)}), bf16[32,2,512,128]{3,1,2,0:T(2,128)(2,1)}, u32[]{:S(2)}, u32[]{:S(2)}) async-start(bf16[32,2,512,128]{3,1,2,0:T(2,128)(2,1)} %copy.44), calls=%async_computation.1 | async-start | bytes 16777216 | tf_op jit(solution)/shard_map/all_to_all | solution.py:71
  349.3 4.6 convolution_convert_fusion
  354.0 7.1 %copy.51 = bf16[32,2,512,128]{3,1,2,0:T(2,128)(2,1)} copy(bf16[32,2,512,128]{3,1,0,2:T(2,128)(2,1)S(1)} %bitcast.54) | data formatting | bytes 16777216 | tf_op jit(solution)/shard_map/reshape | solution.py:64
  361.0 87.9 %all-to-all-done.1 = bf16[32,2,512,128]{3,1,2,0:T(2,128)(2,1)} async-done(((bf16[32,2,512,128]{3,1,2,0:T(2,128)(2,1)}), bf16[32,2,512,128]{3,1,2,0:T(2,128)(2,1)}, u32[]{:S(2)}, u32[]{:S(2)}) %all-to-all-start.1) | async-done | bytes 8388640 | tf_op jit(solution)/shard_map/all_to_all | solution.py:71
  448.9 11.1 %all-to-all-start.3 = ((bf16[32,2,512,128]{3,1,2,0:T(2,128)(2,1)}), bf16[32,2,512,128]{3,1,2,0:T(2,128)(2,1)}, u32[]{:S(2)}, u32[]{:S(2)}) async-start(bf16[32,2,512,128]{3,1,2,0:T(2,128)(2,1)} %copy.51), calls=%async_computation.3 | async-start | bytes 16777216 | tf_op jit(solution)/shard_map/all_to_all | solution.py:73
  460.1 0.1 copy.45
  460.3 8.1 %fusion.14 = bf16[4,512,128]{2,0,1:T(4,128)(2,1)S(1)} fusion(bf16[32,2,512,128]{3,1,2,0:T(2,128)(2,1)} %all-to-all-done.1, bf16[32,2,4]{0,2,1:T(4,128)(2,1)S(1)} %copy.45), kind=kOutput, calls=%fused_computation.12 | convolution fusion | flops 33816576 | bytes 8913408 | tf_op jit(solution)/shard_map/sb,spk->bpk/dot_general | solution.py:80
  468.3 0.4 fusion.19
  468.7 1.3 copy.56
  470.0 89.8 %all-to-all-done.3 = bf16[32,2,512,128]{3,1,2,0:T(2,128)(2,1)} async-done(((bf16[32,2,512,128]{3,1,2,0:T(2,128)(2,1)}), bf16[32,2,512,128]{3,1,2,0:T(2,128)(2,1)}, u32[]{:S(2)}, u32[]{:S(2)}) %all-to-all-start.3) | async-done | bytes 8388640 | tf_op jit(solution)/shard_map/all_to_all | solution.py:73
  559.8 8.0 %fusion.11 = bf16[4,512,128]{2,0,1:T(4,128)(2,1)S(1)} fusion(bf16[32,2,512,128]{3,1,2,0:T(2,128)(2,1)} %all-to-all-done.3, bf16[32,2,4]{0,2,1:T(4,128)(2,1)S(1)} %copy.52), kind=kOutput, calls=%fused_computation.11 | convolution fusion | flops 33816576 | bytes 8913408 | tf_op jit(solution)/shard_map/sb,spk->bpk/dot_general | solution.py:80
  567.9 0.3 fusion.17
  568.2 1.3 copy.57
  (21 shorter events, 0.4 us)
Async XLA Ops:
  7.2 461.2 %copy-start = (bf16[512,128]{1,0:T(8,128)(2,1)S(1)}, bf16[512,128]{1,0:T(8,128)(2,1)}, u32[]{:S(2)}) copy-start(bf16[512,128]{1,0:T(8,128)(2,1)} %param.12) | copy-start | bytes 393220
  7.2 276.7 %all-gather.2.cloned.1.call-start = ((), (), s32[]{:S(2)}) async-start(), calls=%async_computation.4 | async-start | bytes 30670848 | tf_op jit(solution)/shard_map/all_gather | solution.py:34
  9.8 8.6 %copy-start.2 = (s32[26]{0:T(128)}, s32[26]{0:T(128)S(1)}, u32[]{:S(2)}) copy-start(s32[26]{0:T(128)S(1)} %add_add_fusion.1) | copy-start | bytes 316
  10.8 312.0 %all-to-all-start = ((bf16[32,2,4]{2,1,0:T(2,128)(2,1)}), bf16[32,2,4]{2,1,0:T(2,128)(2,1)S(1)}, u32[]{:S(2)}, u32[]{:S(2)}) async-start(bf16[32,2,4]{2,1,0:T(2,128)(2,1)} %bitcast.2), calls=%async_computation | async-start | bytes 32768 | tf_op jit(solution)/shard_map/all_to_all | solution.py:72
  18.7 265.2 %copy-start.3 = (s32[26]{0:T(128)}, s32[26]{0:T(128)S(1)}, u32[]{:S(2)}) copy-start(s32[26]{0:T(128)S(1)} %add_add_fusion) | copy-start | bytes 316
  322.7 19.1 %all-to-all-start.2 = ((bf16[32,2,4]{2,1,0:T(2,128)(2,1)}), bf16[32,2,4]{2,1,0:T(2,128)(2,1)S(1)}, u32[]{:S(2)}, u32[]{:S(2)}) async-start(bf16[32,2,4]{2,1,0:T(2,128)(2,1)} %bitcast.62), calls=%async_computation.2 | async-start | bytes 32768 | tf_op jit(solution)/shard_map/all_to_all | solution.py:74
  341.9 7.5 %copy-start.4 = (s32[26]{0:T(128)S(1)}, s32[26]{0:T(128)}, u32[]{:S(2)}) copy-start(s32[26]{0:T(128)} %copy-done.3) | copy-start | bytes 316
  341.9 107.1 %all-to-all-start.1 = ((bf16[32,2,512,128]{3,1,2,0:T(2,128)(2,1)}), bf16[32,2,512,128]{3,1,2,0:T(2,128)(2,1)}, u32[]{:S(2)}, u32[]{:S(2)}) async-start(bf16[32,2,512,128]{3,1,2,0:T(2,128)(2,1)} %copy.44), calls=%async_computation.1 | async-start | bytes 16777216 | tf_op jit(solution)/shard_map/all_to_all | solution.py:71
  448.9 110.9 %all-to-all-start.3 = ((bf16[32,2,512,128]{3,1,2,0:T(2,128)(2,1)}), bf16[32,2,512,128]{3,1,2,0:T(2,128)(2,1)}, u32[]{:S(2)}, u32[]{:S(2)}) async-start(bf16[32,2,512,128]{3,1,2,0:T(2,128)(2,1)} %copy.51), calls=%async_computation.3 | async-start | bytes 16777216 | tf_op jit(solution)/shard_map/all_to_all | solution.py:73
  468.3 99.5 %copy-start.1 = (bf16[512,128]{1,0:T(8,128)(2,1)S(1)}, bf16[512,128]{1,0:T(8,128)(2,1)}, u32[]{:S(2)}) copy-start(bf16[512,128]{1,0:T(8,128)(2,1)} %param.13) | copy-start | bytes 393220
Sparse Core Ops, SparseCore 0:
  9.8 273.9 all-gather.1
where the time goes:
time: 581 us; the launch traced here: 576 us
  waiting for transfers between devices  442 us (76%)
  matrix products  51.2 us (9%)
  local copies, waits for them, and re-layouts  34.2 us (6%)
  starting transfers between devices  33.7 us (6%)
  between operations  14.2 us (2%)
    all_gather x1, waiting for transfers between devices, shards(): lax.all_gather(transformed, 'aux', axis=0, tiled=True)  263 us
    all_to_all x1, waiting for transfers between devices, shards(): lax.all_to_all(send_col, 'tile', split_axis=0, concat_axis=0, tiled=True)  89.8 us
    all_to_all x1, waiting for transfers between devices, shards(): lax.all_to_all(send_row, 'tile', split_axis=0, concat_axis=0, tiled=True)  87.9 us
    dot_general x1, matrix products, shards(): jnp.dot(masked, lax.all_gather(transformed, 'aux', axis=0, tiled=True), p...  24.6 us
    dot_general x2, matrix products, contract(): jnp.einsum('sb,spk->bpk', weights, flat, preferred_element_type=jnp.float32)  16.1 us
    reshape x2, local copies, waits for them, and re-layouts, pack(): packed.reshape(n_tile, capacity, aux_dev, width)  14.1 us
  transfers between devices with their start and end apart: 5, of which 3 were waited for; matrix products, arithmetic and copies ran while one was open for 13% of the time, Pallas kernels for 0%

commit v1 on v0

--- a/solution.py
+++ b/solution.py
@@ -29,12 +29,7 @@
     )
     masked = coupling * expanded
     pairs = transformed.shape[1]
-    summed = jnp.dot(
-        masked,
-        lax.all_gather(transformed, "aux", axis=0, tiled=True),
-        preferred_element_type=jnp.float32,
-    )
-    gtiles = summed.astype(jnp.bfloat16)
+    gtiles = transformed
     width = density_row.shape[1]
     tiles_dev = pairs // width
     blk_dev = density_row.shape[0] // width
@@ -77,11 +72,16 @@
     def contract(received, marks, density):
         flat = received.reshape(n_tile * capacity, aux_dev, width)
         weights = marks.reshape(n_tile * capacity, blk_dev)
-        totals = jnp.einsum(
-            "sb,spk->bpk", weights, flat, preferred_element_type=jnp.float32
+        sums = jnp.einsum(
+            "sb,spk->pbk", weights, flat, preferred_element_type=jnp.float32
         ).astype(jnp.bfloat16)
+        gathered = lax.all_gather(
+            sums.reshape(aux_dev, blk_dev * width), "aux", axis=0, tiled=True
+        )
+        totals = jnp.dot(masked, gathered, preferred_element_type=jnp.float32)
+        totals = totals.astype(jnp.bfloat16).reshape(aux_dev, blk_dev, width)
         dens = density.reshape(blk_dev, width, width)
-        result = jnp.einsum("bph,bhk->pbk", totals, dens, preferred_element_type=jnp.float32)
+        result = jnp.einsum("pbh,bhk->pbk", totals, dens, preferred_element_type=jnp.float32)
         return result.reshape(aux_dev, blk_dev * width)
 
     grad_row = contract(recv_row, got_row, density_row)

time: 581 us -> 354 us (0.61)
  waiting for transfers between devices: 442 us -> 224 us
  matrix products: 51.2 us -> 41.4 us
    all_gather x1 -> x2, waiting for transfers between devices: 263 us -> 46.2 us  [contract(): lax.all_gather(sums.reshape(aux_dev, blk_dev * width), 'aux', axis=0, til...]
    dot_general x5 -> x6, matrix products: 41.4 us -> 31 us  [the longest x2 16 us: contract(): jnp.einsum('sb,spk->pbk', weights, flat, preferred_element_type=jnp.float32)]
    unnamed x12 -> x19, local copies, waits for them, and re-layouts: 2.64 us -> 9.24 us
  transfers between devices with their start and end apart: 5 -> 6, of which waited for: 3 -> 3; matrix products, arithmetic and copies ran while one was open for 13% -> 19% of each run, Pallas kernels for 0% -> 0%
where the time goes in v1:
time: 354 us; the launch traced here: 353 us
  waiting for transfers between devices  224 us (63%)
  matrix products  41.4 us (12%)
  local copies, waits for them, and re-layouts  37.4 us (11%)
  starting transfers between devices  33.8 us (10%)
  between operations  14.2 us (4%)
    all_to_all x1, waiting for transfers between devices, shards(): lax.all_to_all(send_col, 'tile', split_axis=0, concat_axis=0, tiled=True)  90.3 us
    all_to_all x1, waiting for transfers between devices, shards(): lax.all_to_all(send_row, 'tile', split_axis=0, concat_axis=0, tiled=True)  87.9 us
    all_gather x2, waiting for transfers between devices, contract(): lax.all_gather(sums.reshape(aux_dev, blk_dev * width), 'aux', axis=0, til...  46.2 us
    dot_general x2, matrix products, contract(): jnp.einsum('sb,spk->pbk', weights, flat, preferred_element_type=jnp.float32)  16 us
    dot_general x2, matrix products, contract(): totals = jnp.dot(masked, gathered, preferred_element_type=jnp.float32)  14.3 us
    reshape x2, local copies, waits for them, and re-layouts, pack(): packed.reshape(n_tile, capacity, aux_dev, width)  14.1 us
    all_to_all x1, starting transfers between devices, shards(): lax.all_to_all(send_col, 'tile', split_axis=0, concat_axis=0, tiled=True)  11.1 us
    dot_general x2, matrix products, pack(): jnp.einsum('st,ptk->spk', place, three, preferred_element_type=jnp.float32)  9.27 us
  transfers between devices with their start and end apart: 6, of which 3 were waited for; matrix products, arithmetic and copies ran while one was open for 19% of the time, Pallas kernels for 0%

profile of v1, /device:TPU:2, one launch (start us, length us, event | category | flops | bytes accessed | tf_op | source)
XLA Modules:
  0.0 352.6 jit_solution(16813108567842337471)
XLA Ops:
  7.2 0.8 fusion.30
  8.3 0.8 fusion.32
  9.1 0.2 convolution_convert_fusion.5
  9.3 0.7 copy.39
  10.1 7.6 %all-to-all-start.1 = ((bf16[32,2,4]{2,1,0:T(2,128)(2,1)}), bf16[32,2,4]{2,1,0:T(2,128)(2,1)S(1)}, u32[]{:S(2)}, u32[]{:S(2)}) async-start(bf16[32,2,4]{2,1,0:T(2,128)(2,1)} %bitcast.6), calls=%async_computation.1 | async-start | bytes 32768 | tf_op jit(solution)/shard_map/all_to_all | solution.py:67
  18.0 0.6 copy-done.4
  18.6 0.8 convolution_convert_fusion.4
  19.4 4.2 %copy.36 = bf16[512,3328]{0,1:T(8,128)(2,1)S(1)} copy(bf16[512,3328]{1,0:T(8,128)(2,1)} %param.9) | data formatting | bytes 6815744 | tf_op args[0]
  23.7 6.3 %copy.37 = bf16[512,26,128]{2,1,0:T(8,128)(2,1)} copy(bf16[512,26,128]{0,2,1:T(8,128)(2,1)S(1)} %bitcast.72) | data formatting | bytes 6815744 | tf_op jit(solution)/shard_map/reshape | solution.py:37
  30.0 1.4 copy.46
  31.3 7.4 %all-to-all-start.3 = ((bf16[32,2,4]{2,1,0:T(2,128)(2,1)}), bf16[32,2,4]{2,1,0:T(2,128)(2,1)S(1)}, u32[]{:S(2)}, u32[]{:S(2)}) async-start(bf16[32,2,4]{2,1,0:T(2,128)(2,1)} %bitcast.19), calls=%async_computation.3 | async-start | bytes 32768 | tf_op jit(solution)/shard_map/all_to_all | solution.py:69
  38.7 4.6 %convolution_convert_fusion.1 = bf16[64,512,128]{2,0,1:T(8,128)(2,1)S(1)} fusion(bf16[512,26,128]{2,1,0:T(8,128)(2,1)} %copy.37, s32[26]{0:T(128)} %copy-done.3), kind=kOutput, calls=%fused_computation.5 | convolution fusion | flops 222299776 | bytes 11796584 | tf_op jit(solution)/shard_map/st,ptk->spk/dot_general | solution.py:51
  43.4 7.0 %copy.38 = bf16[32,2,512,128]{3,1,2,0:T(2,128)(2,1)} copy(bf16[32,2,512,128]{3,1,0,2:T(2,128)(2,1)S(1)} %bitcast.71) | data formatting | bytes 16777216 | tf_op jit(solution)/shard_map/reshape | solution.py:59
  50.4 7.4 %all-to-all-start = ((bf16[32,2,512,128]{3,1,2,0:T(2,128)(2,1)}), bf16[32,2,512,128]{3,1,2,0:T(2,128)(2,1)}, u32[]{:S(2)}, u32[]{:S(2)}) async-start(bf16[32,2,512,128]{3,1,2,0:T(2,128)(2,1)} %copy.38), calls=%async_computation | async-start | bytes 16777216 | tf_op jit(solution)/shard_map/all_to_all | solution.py:66
  57.8 4.6 %convolution_convert_fusion = bf16[64,512,128]{2,0,1:T(8,128)(2,1)S(1)} fusion(bf16[512,26,128]{2,1,0:T(8,128)(2,1)} %copy.37, s32[26]{0:T(128)S(1)} %copy-done.5), kind=kOutput, calls=%fused_computation.4 | convolution fusion | flops 222299776 | bytes 11796584 | tf_op jit(solution)/shard_map/st,ptk->spk/dot_general | solution.py:51
  62.5 7.1 %copy.45 = bf16[32,2,512,128]{3,1,2,0:T(2,128)(2,1)} copy(bf16[32,2,512,128]{3,1,0,2:T(2,128)(2,1)S(1)} %bitcast.70) | data formatting | bytes 16777216 | tf_op jit(solution)/shard_map/reshape | solution.py:59
  69.6 87.9 %all-to-all-done = bf16[32,2,512,128]{3,1,2,0:T(2,128)(2,1)} async-done(((bf16[32,2,512,128]{3,1,2,0:T(2,128)(2,1)}), bf16[32,2,512,128]{3,1,2,0:T(2,128)(2,1)}, u32[]{:S(2)}, u32[]{:S(2)}) %all-to-all-start) | async-done | bytes 8388640 | tf_op jit(solution)/shard_map/all_to_all | solution.py:66
  157.5 11.1 %all-to-all-start.2 = ((bf16[32,2,512,128]{3,1,2,0:T(2,128)(2,1)}), bf16[32,2,512,128]{3,1,2,0:T(2,128)(2,1)}, u32[]{:S(2)}, u32[]{:S(2)}) async-start(bf16[32,2,512,128]{3,1,2,0:T(2,128)(2,1)} %copy.45), calls=%async_computation.2 | async-start | bytes 16777216 | tf_op jit(solution)/shard_map/all_to_all | solution.py:68
  168.9 8.0 %fusion.13 = bf16[512,128,4]{1,2,0:T(4,128)(2,1)S(1)} fusion(bf16[32,2,512,128]{3,1,2,0:T(2,128)(2,1)} %all-to-all-done, bf16[32,2,4]{0,2,1:T(4,128)(2,1)S(1)} %copy.41), kind=kOutput, calls=%fused_computation.10 | convolution fusion | flops 33816576 | bytes 8913408 | tf_op jit(solution)/shard_map/sb,spk->pbk/dot_general | solution.py:75
  176.9 0.9 copy.80
  178.0 90.3 %all-to-all-done.2 = bf16[32,2,512,128]{3,1,2,0:T(2,128)(2,1)} async-done(((bf16[32,2,512,128]{3,1,2,0:T(2,128)(2,1)}), bf16[32,2,512,128]{3,1,2,0:T(2,128)(2,1)}, u32[]{:S(2)}, u32[]{:S(2)}) %all-to-all-start.2) | async-done | bytes 8388640 | tf_op jit(solution)/shard_map/all_to_all | solution.py:68
  268.3 8.0 %fusion.10 = bf16[512,128,4]{1,2,0:T(4,128)(2,1)S(1)} fusion(bf16[32,2,512,128]{3,1,2,0:T(2,128)(2,1)} %all-to-all-done.2, bf16[32,2,4]{0,2,1:T(4,128)(2,1)S(1)} %copy.48), kind=kOutput, calls=%fused_computation.9 | convolution fusion | flops 33816576 | bytes 8913408 | tf_op jit(solution)/shard_map/sb,spk->pbk/dot_general | solution.py:75
  276.3 0.9 copy.79
  277.3 0.7 dynamic-slice_convert_fusion
  278.0 3.9 %broadcast_in_dim.5 = bf16[512,32,128]{2,1,0:T(8,128)(2,1)S(1)} broadcast(bf16[512,32]{1,0:T(8,128)(2,1)S(1)} %bitcast.79), dimensions={0,1} | broadcast | bytes 4227072 | tf_op jit(solution)/shard_map/broadcast_in_dim | solution.py:27
  281.9 6.7 %convolution_convert_fusion.3 = bf16[512,512]{0,1:T(8,128)(2,1)S(1)} fusion(bf16[4096,512]{1,0:T(8,128)(2,1)} %all-gather.3.cloned.1.call-done, bf16[512,4096]{1,0:T(8,128)(2,1)S(1)} %copy-done.6, bf16[64,8,32,128]{3,2,1,0:T(8,128)(2,1)S(1)} %bitcast.73), kind=kOutput, calls=%fused_computation.12 | convolution fusion | flops 2149842944 | bytes 13107200 | tf_op jit(solution)/shard_map/dot_general | solution.py:81
  288.6 0.3 fusion.34
  289.0 1.3 copy.51
  290.3 46.2 %all-gather.5.cloned.1.call-done = bf16[4096,512]{1,0:T(8,128)(2,1)} async-done(((bf16[512,512]{1,0:T(8,128)(2,1)}), bf16[4096,512]{1,0:T(8,128)(2,1)}) %all-gather.5.cloned.1.call-update) | async-done | bytes 4194320 | tf_op jit(solution)/shard_map/all_gather | solution.py:78
  336.5 7.6 %convolution_convert_fusion.2 = bf16[512,512]{0,1:T(8,128)(2,1)S(1)} fusion(bf16[4096,512]{1,0:T(8,128)(2,1)} %all-gather.5.cloned.1.call-done, bf16[512,4096]{1,0:T(8,128)(2,1)} %param.10, bf16[64,8,32,128]{3,2,1,0:T(8,128)(2,1)} %bitcast.74), kind=kOutput, calls=%fused_computation.11 | convolution fusion | flops 2149842944 | bytes 13107200 | tf_op jit(solution)/shard_map/dot_general | solution.py:81
  344.1 0.3 fusion.35
  344.5 1.3 copy.52
  (31 shorter events, 1.2 us)
Async XLA Ops:
  7.2 281.5 %copy-start = (bf16[512,128]{1,0:T(8,128)(2,1)S(1)}, bf16[512,128]{1,0:T(8,128)(2,1)}, u32[]{:S(2)}) copy-start(bf16[512,128]{1,0:T(8,128)(2,1)} %param.12) | copy-start | bytes 393220
  8.3 9.4 %copy-start.3 = (s32[26]{0:T(128)}, s32[26]{0:T(128)S(1)}, u32[]{:S(2)}) copy-start(s32[26]{0:T(128)S(1)} %add_add_fusion.1) | copy-start | bytes 316
  10.1 21.3 %all-to-all-start.1 = ((bf16[32,2,4]{2,1,0:T(2,128)(2,1)}), bf16[32,2,4]{2,1,0:T(2,128)(2,1)S(1)}, u32[]{:S(2)}, u32[]{:S(2)}) async-start(bf16[32,2,4]{2,1,0:T(2,128)(2,1)} %bitcast.6), calls=%async_computation.1 | async-start | bytes 32768 | tf_op jit(solution)/shard_map/all_to_all | solution.py:67
  18.0 0.6 copy-start.4
  31.3 19.1 %all-to-all-start.3 = ((bf16[32,2,4]{2,1,0:T(2,128)(2,1)}), bf16[32,2,4]{2,1,0:T(2,128)(2,1)S(1)}, u32[]{:S(2)}, u32[]{:S(2)}) async-start(bf16[32,2,4]{2,1,0:T(2,128)(2,1)} %bitcast.19), calls=%async_computation.3 | async-start | bytes 32768 | tf_op jit(solution)/shard_map/all_to_all | solution.py:69
  50.4 7.5 %copy-start.5 = (s32[26]{0:T(128)S(1)}, s32[26]{0:T(128)}, u32[]{:S(2)}) copy-start(s32[26]{0:T(128)} %copy-done.4) | copy-start | bytes 316
  50.4 107.1 %all-to-all-start = ((bf16[32,2,512,128]{3,1,2,0:T(2,128)(2,1)}), bf16[32,2,512,128]{3,1,2,0:T(2,128)(2,1)}, u32[]{:S(2)}, u32[]{:S(2)}) async-start(bf16[32,2,512,128]{3,1,2,0:T(2,128)(2,1)} %copy.38), calls=%async_computation | async-start | bytes 16777216 | tf_op jit(solution)/shard_map/all_to_all | solution.py:66
  157.5 110.9 %all-to-all-start.2 = ((bf16[32,2,512,128]{3,1,2,0:T(2,128)(2,1)}), bf16[32,2,512,128]{3,1,2,0:T(2,128)(2,1)}, u32[]{:S(2)}, u32[]{:S(2)}) async-start(bf16[32,2,512,128]{3,1,2,0:T(2,128)(2,1)} %copy.45), calls=%async_computation.2 | async-start | bytes 16777216 | tf_op jit(solution)/shard_map/all_to_all | solution.py:68
  168.6 109.3 %all-gather.3.cloned.1.call-start = ((), (), s32[]{:S(2)}) async-start(), calls=%async_computation.4 | async-start | bytes 4718592 | tf_op jit(solution)/shard_map/all_gather | solution.py:78
  177.8 158.6 %all-gather.5.cloned.1.call-start = ((), (), s32[]{:S(2)}) async-start(), calls=%async_computation.5 | async-start | bytes 4718592 | tf_op jit(solution)/shard_map/all_gather | solution.py:78
  278.0 4.0 %copy-start.6 = (bf16[512,4096]{1,0:T(8,128)(2,1)S(1)}, bf16[512,4096]{1,0:T(8,128)(2,1)}, u32[]{:S(2)}) copy-start(bf16[512,4096]{1,0:T(8,128)(2,1)} %param.10) | copy-start | bytes 12582916
  281.9 6.7 %copy-start.1 = (bf16[512,32,128]{2,1,0:T(8,128)(2,1)}, bf16[512,32,128]{2,1,0:T(8,128)(2,1)S(1)}, u32[]{:S(2)}) copy-start(bf16[512,32,128]{2,1,0:T(8,128)(2,1)S(1)} %broadcast_in_dim.5) | copy-start | bytes 12582916
  290.3 53.8 %copy-start.2 = (bf16[512,128]{1,0:T(8,128)(2,1)S(1)}, bf16[512,128]{1,0:T(8,128)(2,1)}, u32[]{:S(2)}) copy-start(bf16[512,128]{1,0:T(8,128)(2,1)} %param.13) | copy-start | bytes 393220
Sparse Core Ops, SparseCore 0:
  178.0 57.6 all-gather.2
  277.4 59.0 all-gather.4

commit v2 on v1

v2 whole, which is shorter than its diff:
```python
import functools

import jax
import jax.numpy as jnp
from jax import lax
from jax.experimental import pallas as pl
from jax.experimental.pallas import tpu as pltpu
from jax.sharding import PartitionSpec as P

RING = 4
CORES = 2
W = 128
CHUNKS = ((0, 0, 128), (1, 0, 128), (2, 0, 128), (3, 0, 128))
SUBS = 2
F32, BF16 = jnp.float32, jnp.bfloat16


def kernel(nz, tiles, tbl, mask, t_hbm, c_hbm, dr, dc, out_r, out_c, *scratch):
    n = len(CHUNKS)
    groups = c_hbm.shape[1] // (nz * W)
    it = iter(scratch)
    take = lambda k: [next(it) for _ in range(k)]
    raw, rest, sa, ra, sb, rb, us = (take(n) for _ in range(7))
    uz = take(groups)
    amat = take(groups)
    own, total = take(2)
    (a_sem, loc_sem, e1_send, sib_send, e1_recv, fw_send, ea_send, ea_recv, eb_send, eb_recv,
     es_send, es_recv, z_send, z_recv) = take(14)

    z, t = lax.axis_index("aux"), lax.axis_index("tile")
    c, x, y = t % CORES, (t // CORES) % RING, t // (CORES * RING)

    def tid(yy, xx, cc):
        return (yy * RING + xx) * CORES + cc

    def pick(for0, for1):
        return for0 + c * (for1 - for0)

    def first(d):
        return pick(tid(y, (x + RING + d) % RING, 0), tid((y + RING + d) % RING, x, 1))

    def crossed(d):
        return pick(tid((y + RING + d) % RING, x, 1), tid(y, (x + RING + d) % RING, 0))

    def second(d):
        return pick(tid((y + RING + d) % RING, x, 0), tid(y, (x + RING + d) % RING, 1))

    sibling = tid(y, x, 1 - c)
    m2 = pick(y, x)
    g_opp, g_p, g_m = (m2 + 2) % RING, (m2 + 1) % RING, (m2 + 3) % RING
    z_to = ((z + 1) % nz, (z + nz - 1) % nz)
    sent = []

    def remote(src, dst, send, recv, zz, tt):
        return pltpu.make_async_remote_copy(
            src_ref=src, dst_ref=dst, send_sem=send, recv_sem=recv,
            device_id=(zz, tt), device_id_type=pl.DeviceIdType.MESH)

    def go(src, dst, send, recv, zz, tt):
        copy = remote(src, dst, send, recv, zz, tt)
        copy.start()
        sent.append(copy)

    def arrived(ref, recv):
        remote(ref, ref, a_sem.at[0], recv, z, sibling).wait_recv()

    def rows_of(i, h):
        g, off, rows = CHUNKS[i]
        return pl.ds(pl.multiple_of(g * W + off + h * (rows // 2), 16), rows // 2)

    def slot(i, s):
        return raw[i].at[s, pl.ds(0, tiles)]

    def load_raw(i):
        for k, (h, to) in enumerate(((c, slot(i, c)), (1 - c, rest[i]))):
            def body(e, carry, h=h, to=to, k=k):
                pltpu.make_async_copy(
                    t_hbm.at[rows_of(i, h), pl.ds(pl.multiple_of(e * W, W), W)],
                    to.at[e], loc_sem.at[i, k]).start()
                return carry

            lax.fori_loop(0, tiles, body, 0)

    for i in range(n):
        load_raw(i)

    a_copies = []
    for g in range(groups):
        for b in range(nz):
            copy = pltpu.make_async_copy(
                c_hbm.at[:, pl.ds((b * groups + g) * W, W)],
                amat[g].at[:, pl.ds(b * W, W)], a_sem.at[g])
            copy.start()
            a_copies.append(copy)
    for i in range(n):
        for s in range(2 * RING):
            raw[i][s, tiles] = jnp.zeros(raw[i].shape[2:], BF16)

    barrier = pltpu.get_barrier_semaphore()
    near = [(z, sibling), (z_to[0], t), (z_to[1], t)]
    for d in (1, -1):
        for cc in range(CORES):
            near.append((z, tid(y, (x + RING + d) % RING, cc)))
            near.append((z, tid((y + RING + d) % RING, x, cc)))
    for who in near:
        pl.semaphore_signal(barrier, inc=1, device_id=who, device_id_type=pl.DeviceIdType.MESH)
    pl.semaphore_wait(barrier, len(near))

    def start_raw(i):
        for k, (src, to) in enumerate(((slot(i, c), first), (rest[i], crossed))):
            pltpu.make_async_copy(src, src, loc_sem.at[i, k]).wait()
            for m, d in enumerate((1, -1)):
                s = ((RING - d) % RING) * CORES + c
                go(src, slot(i, s), e1_send.at[i, 2 * k + m], e1_recv.at[i, s], z, to(d))
        go(rest[i], slot(i, c), sib_send.at[i], e1_recv.at[i, c], z, sibling)

    def forward_raw(i):
        for d, s in ((1, 6), (-1, 3)):
            arrived(slot(i, s), e1_recv.at[i, s])
            to = 2 * CORES + (0 if d == 1 else 1)
            go(slot(i, s), slot(i, to), fw_send.at[i, 0 if d == 1 else 1], e1_recv.at[i, to],
               z, first(d))

    def finish_raw(i):
        arrived(slot(i, 1 - c), e1_recv.at[i, 1 - c])
        for s in (2, 7, 4, 5):
            arrived(slot(i, s), e1_recv.at[i, s])

    def summed(i, g, j):
        acc = None
        for e in range(4 * RING):
            v = raw[i][e // 2, tbl[(g * 16 + j) * 16 + e]].astype(F32)
            acc = v if acc is None else acc + v
        return acc

    def fill(i, g, low, high, store, extra=None):
        def body(j, carry):
            v = summed(i, g, j)
            if extra is not None:
                v = v + extra[j - low].astype(F32)
            store[j] = v.astype(store.dtype)
            return carry

        lax.fori_loop(low, high, body, 0)

    def scatter_a(i):
        fill(i, g_opp, 0, 16, sa[i])
        go(sa[i].at[pl.ds(0, 8)], ra[i].at[0], ea_send.at[i, 0], ea_recv.at[i, 0], z, second(1))
        go(sa[i].at[pl.ds(8, 8)], ra[i].at[1], ea_send.at[i, 1], ea_recv.at[i, 1], z, second(-1))

    def scatter_b(i):
        fill(i, g_p, 8, 16, sb[i].at[0])
        fill(i, g_m, 0, 8, sb[i].at[1])
        arrived(ra[i].at[0], ea_recv.at[i, 0])
        fill(i, g_p, 0, 8, sb[i].at[0], ra[i].at[0])
        go(sb[i].at[0], rb[i].at[0], eb_send.at[i, 0], eb_recv.at[i, 0], z, second(1))
        arrived(ra[i].at[1], ea_recv.at[i, 1])
        fill(i, g_m, 8, 16, sb[i].at[1], ra[i].at[1])
        go(sb[i].at[1], rb[i].at[1], eb_send.at[i, 1], eb_recv.at[i, 1], z, second(-1))
        fill(i, m2, 0, 16, own)

    def part(i, zz, first_row, rows):
        g, off, _ = CHUNKS[i]
        return uz[g].at[zz, pl.ds(pl.multiple_of(off + first_row, 16), rows)]

    def owners(i):
        g, off, rows = CHUNKS[i]
        half = rows // 2
        mine = pl.ds(pl.multiple_of(off + c * half, 16), half)
        for k in range(2):
            arrived(rb[i].at[k], eb_recv.at[i, k])

        def position(j):
            return own[j] + rb[i][0, j].astype(F32) + rb[i][1, j].astype(F32)

        for jj in range(8):
            us[i][:, jj * W:(jj + 1) * W] = position((1 - c) * 8 + jj).astype(BF16)
        go(us[i], part(i, z, c * half, half), es_send.at[i], es_recv.at[i], z, sibling)
        for jj in range(8):
            uz[g][z, mine, jj * W:(jj + 1) * W] = position(c * 8 + jj).astype(BF16)

    def z_copy(i, k, step, q):
        rows = CHUNKS[i][2] // SUBS
        origin = (z + (nz - step if k == 0 else step)) % nz
        ref = part(i, origin, q * rows, rows)
        go(ref, ref, z_send.at[i, k, step * SUBS + q], z_recv.at[i, k, step * SUBS + q],
           z_to[k], t)

    def z_wait(i, k, step, q):
        rows = CHUNKS[i][2] // SUBS
        origin = (z + (2 * nz - 1 - step if k == 0 else step + 1)) % nz
        arrived(part(i, origin, q * rows, rows), z_recv.at[i, k, step * SUBS + q])

    def z_begin(i):
        half = CHUNKS[i][2] // 2
        arrived(part(i, z, (1 - c) * half, half), es_recv.at[i])
        for q in range(SUBS):
            for k in range(2):
                z_copy(i, k, 0, q)

    last = nz // 2 - 1

    def z_forward(i, step):
        for q in range(SUBS):
            for k in range(2):
                z_wait(i, k, step - 1, q)
                if step < last or (q * 2 // SUBS) == k:
                    z_copy(i, k, step, q)

    def z_end(i):
        for q in range(SUBS):
            z_wait(i, q * 2 // SUBS, last, q)

    def masked():
        for copy in a_copies:
            copy.wait()
        rows = amat[0].shape[0] // W
        for g in range(groups):
            def body(e, carry):
                b, p = e // rows, e % rows
                keep = mask[z * rows + p, b * groups + g].astype(F32)
                at = (pl.ds(pl.multiple_of(p * W, W), W), pl.ds(pl.multiple_of(b * W, W), W))
                amat[g][at] = (amat[g][at].astype(F32) * keep).astype(BF16)
                return carry

            lax.fori_loop(0, nz * rows, body, 0)

    step_n = 256

    def product(g):
        def body(e, carry):
            at = pl.ds(pl.multiple_of(e * step_n, step_n), step_n)
            right = uz[g][:, :, at].reshape(nz * W, step_n)
            new = jnp.dot(amat[g][...], right, preferred_element_type=F32)
            if g > 0:
                new = new + total[:, at]
            total[:, at] = new
            return carry

        lax.fori_loop(0, total.shape[1] // step_n, body, 0)

    def done_group(i):
        g, off, rows = CHUNKS[i]
        return g if off + rows == W else None

    start_raw(0)
    masked()
    forward_raw(0)
    finish_raw(0)
    if n > 1:
        start_raw(1)
    for i in range(n):
        scatter_a(i)
        if i > 0:
            z_forward(i - 1, 1)
        scatter_b(i)
        if i + 1 < n:
            forward_raw(i + 1)
        if i > 0:
            z_forward(i - 1, 2)
        owners(i)
        if i > 0:
            z_forward(i - 1, 3)
        z_begin(i)
        if i + 1 < n:
            finish_raw(i + 1)
        if i + 2 < n:
            start_raw(i + 2)
        if i > 0:
            z_end(i - 1)
            if done_group(i - 1) is not None:
                product(done_group(i - 1))
    for s in (1, 2, 3):
        z_forward(n - 1, s)
    z_end(n - 1)
    product(done_group(n - 1))

    blocks = dr.shape[0] // W
    for k, (dens, out) in enumerate(((dr, out_r), (dc, out_c))):
        for b in range(blocks):
            at = (k * blocks + b) * W
            s = total[:, at:at + W]
            high = s.astype(BF16)
            low = (s - high.astype(F32)).astype(BF16)
            d = dens[b * W:(b + 1) * W, :]
            out[:, b * W:(b + 1) * W] = jnp.dot(high, d, preferred_element_type=F32) + jnp.dot(
                low, d, preferred_element_type=F32)
    for copy in sent:
        copy.wait_send()


def tables(row_owner, row_slot, col_owner, col_slot, slots):
    t = lax.axis_index("tile")
    c, x, y = t % CORES, (t // CORES) % RING, t // (CORES * RING)
    tiles = row_owner.shape[0] // (RING * RING * CORES)
    key = jnp.stack([(row_owner * slots + row_slot)[:, 0], (col_owner * slots + col_slot)[:, 0]])
    key = key.reshape(2, RING, RING, CORES, tiles)
    key = jnp.where(c == 0, lax.dynamic_index_in_dim(key, y, 1, False),
                    lax.dynamic_index_in_dim(key, x, 2, False))
    mine = jnp.where(c == 0, x, y)
    key = lax.dynamic_slice_in_dim(jnp.concatenate([key, key], 1), mine, RING, 1)
    k = jnp.arange(tiles, dtype=jnp.int32)
    earlier = (key[..., None, :] == key[..., :, None]) & (k[None, :] < k[:, None])
    rank = jnp.sum(earlier.astype(jnp.int32), axis=-1)
    g = jnp.arange(RING, dtype=jnp.int32)
    base = jnp.where(c == 0, (g * RING + x) * CORES, (y * RING + g) * CORES)
    want = (base[:, None] + jnp.arange(CORES, dtype=jnp.int32)[None, :])[:, :, None] * slots
    want = want + jnp.arange(slots, dtype=jnp.int32)[None, None, :]
    want = want[:, :, None, :, None, None, None, None]
    hit = (key[None, None, :, None, :, :, None, :] == want) & (
        rank[None, None, :, None, :, :, None, :]
        == jnp.arange(2, dtype=jnp.int32)[None, None, None, None, None, None, :, None])
    spot = jnp.min(jnp.where(hit, k, tiles), axis=-1)
    return spot.reshape(-1)


def shards(transformed, coupling, block_mask, density_row, density_col,
           row_owner, row_slot, col_owner, col_slot):
    nz = lax.axis_size("aux")
    aux_dev, pairs = transformed.shape
    tiles = pairs // W
    slots = density_row.shape[0] // W
    columns = 2 * density_row.shape[0]
    groups = aux_dev // W
    tbl = tables(row_owner, row_slot, col_owner, col_slot, slots)
    n = len(CHUNKS)
    halves = [c[2] // 2 for c in CHUNKS]
    scratch = []
    scratch += [pltpu.VMEM((2 * RING, tiles + 1, h, W), BF16) for h in halves]
    scratch += [pltpu.VMEM((tiles, h, W), BF16) for h in halves]
    scratch += [pltpu.VMEM((16, h, W), BF16) for h in halves]
    scratch += [pltpu.VMEM((2, 8, h, W), BF16) for h in halves]
    scratch += [pltpu.VMEM((2, 16, h, W), BF16) for h in halves]
    scratch += [pltpu.VMEM((2, 16, h, W), BF16) for h in halves]
    scratch += [pltpu.VMEM((h, columns), BF16) for h in halves]
    scratch += [pltpu.VMEM((nz, W, columns), BF16) for _ in range(groups)]
    scratch += [pltpu.VMEM((aux_dev, nz * W), BF16) for _ in range(groups)]
    scratch += [pltpu.VMEM((16, max(halves), W), F32), pltpu.VMEM((aux_dev, columns), F32)]
    dma = pltpu.SemaphoreType.DMA
    steps = nz // 2 * SUBS
    scratch += [dma((groups,)), dma((n, 2)), dma((n, 4)), dma((n,)), dma((n, 8)), dma((n, 2)),
                dma((n, 2)), dma((n, 2)), dma((n, 2)), dma((n, 2)), dma((n,)), dma((n,)),
                dma((n, 2, steps)), dma((n, 2, steps))]
    vmem, smem = pl.BlockSpec(memory_space=pltpu.VMEM), pl.BlockSpec(memory_space=pltpu.SMEM)
    hbm = pl.BlockSpec(memory_space=pl.ANY)
    shape = jax.ShapeDtypeStruct((aux_dev, columns // 2), F32)
    return pl.pallas_call(
        functools.partial(kernel, nz, tiles),
        out_shape=(shape, shape),
        in_specs=[smem, smem, hbm, hbm, vmem, vmem],
        out_specs=(vmem, vmem),
        scratch_shapes=scratch,
        compiler_params=pltpu.CompilerParams(
            collective_id=0, has_side_effects=True, vmem_limit_bytes=56 * 1024 * 1024),
        cost_estimate=pl.CostEstimate(
            flops=2 * aux_dev * nz * aux_dev * columns, bytes_accessed=16 << 20,
            transcendentals=0),
    )(tbl, block_mask, transformed, coupling, density_row, density_col)


def solution(mesh):
    placed = (P("aux", "tile"), P("aux", None), P(), P("tile", None), P("tile", None),
              P(), P(), P(), P())
    return jax.shard_map(shards, mesh=mesh, in_specs=placed,
                         out_specs=(P("aux", "tile"), P("aux", "tile")), check_vma=False)
```

time: 354 us -> 168 us (0.47)
  waiting for transfers between devices: 224 us -> 0 us
  Pallas kernels: 0 us -> 151 us
  matrix products: 41.4 us -> 0 us
  starting transfers between devices: 33.8 us -> 0 us
  local copies, waits for them, and re-layouts: 37.4 us -> 6.8 us
  between operations: 14.2 us -> 0.77 us
  other arithmetic: 1.31 us -> 8.35 us
    all_to_all x4 -> x0, waiting for transfers between devices: 178 us -> none  [the longest x1 90.3 us: shards(): lax.all_to_all(send_col, 'tile', split_axis=0, concat_axis=0, tiled=True)]
    pallas_call x0 -> x1, Pallas kernels: none -> 151 us  [shards(): pl.pallas_call(functools.partial(kernel, nz, tiles), out_shape=(shape, sh...]
    all_gather x2 -> x0, waiting for transfers between devices: 46.2 us -> none  [contract(): lax.all_gather(sums.reshape(aux_dev, blk_dev * width), 'aux', axis=0, til...]
    dot_general x10 -> x0, matrix products: 41.4 us -> none  [the longest x2 16 us: contract(): jnp.einsum('sb,spk->pbk', weights, flat, preferred_element_type=jnp.float32)]
    all_to_all x4 -> x0, starting transfers between devices: 33.6 us -> none  [the longest x1 11.1 us: shards(): lax.all_to_all(send_col, 'tile', split_axis=0, concat_axis=0, tiled=True)]
    reshape x3 -> x1, local copies, waits for them, and re-layouts: 20.4 us -> 0.92 us  [tables(): return spot.reshape(-1)]
    unnamed x19 -> x3, local copies, waits for them, and re-layouts: 9.24 us -> 4.53 us
    reduce_min x0 -> x1, other arithmetic: none -> 4.6 us  [tables(): spot = jnp.min(jnp.where(hit, k, tiles), axis=-1)]
  transfers between devices with their start and end apart: 6 -> 0, of which waited for: 3 -> 0; matrix products, arithmetic and copies ran while one was open for 19% -> 0% of each run, Pallas kernels for 0% -> 0%
where the time goes in v2:
time: 168 us; the launch traced here: 167 us
  Pallas kernels  151 us (90%)
  other arithmetic  8.35 us (5%)
  local copies, waits for them, and re-layouts  6.8 us (4%)
    pallas_call x1, Pallas kernels, shards(): pl.pallas_call(functools.partial(kernel, nz, tiles), out_shape=(shape, sh...  151 us
    reduce_min x1, other arithmetic, tables(): spot = jnp.min(jnp.where(hit, k, tiles), axis=-1)  4.6 us
    unnamed x3, local copies, waits for them, and re-layouts  4.53 us

profile of v2, /device:TPU:2, one launch (start us, length us, event | category | flops | bytes accessed | tf_op | source)
XLA Modules:
  0.0 167.0 jit_solution(4572643016906995209)
XLA Ops:
  0.7 0.1 add_multiply_fusion
  0.8 0.1 iota_add_fusion
  0.8 0.7 add_reduce_fusion.1
  1.6 0.7 add_reduce_fusion
  2.3 0.1 stack.8
  2.4 0.1 stack.7
  2.6 0.1 copy.20
  2.8 2.0 %convert_reduce_fusion = s32[2,4,2,26]{1,3,2,0:T(8,128)S(1)} fusion(s32[2,4,2,26]{1,3,2,0:T(8,128)S(1)} %copy.20, s32[2,4,2,26]{3,1,2,0:T(4,128)S(1)} %copy.18, pred[26,26]{1,0:T(8,128)(4,1)S(1)} %iota_compare_fusion.1), kind=kLoop, calls=%fused_computation.1 | loop fusion | flops 42848 | bytes 5668 | tf_op jit(solution)/shard_map/reduce_sum | solution.py:304
  4.7 0.1 copy.21
  4.8 0.1 broadcast_compare_fusion
  5.0 4.6 %select_reduce_fusion = s32[4,2,2,4,4,2,2]{4,6,5,3,2,1,0:T(2,128)S(1)} fusion(pred[2,4,2,2,26]{4,1,3,2,0:T(4,128)(4,1)S(1)} %iota_compare_fusion, pred[4,2,2,4,4,2,26]{6,4,5,3,2,1,0:T(4,128)(4,1)S(1)} %broadcast_compare_fusion), kind=kLoop, calls=%fused_computation | loop fusion | flops 78848 | bytes 18240 | tf_op jit(solution)/shard_map/reduce_min | solution.py:313
  9.6 0.9 copy.22
  10.5 0.9 reshape.76.tbl
  11.4 151.0 %shard_map.104 = (f32[512,512]{1,0:T(8,128)}, f32[512,512]{1,0:T(8,128)}) custom-call(s32[1024]{0:T(1024)} %reshape.76.tbl, s32[32,32]{1,0:T(8,128)} %mask.1, bf16[512,3328]{1,0:T(8,128)(2,1)} %t_hbm.1, bf16[512,4096]{1,0:T(8,128)(2,1)} %c_hbm.1, bf16[512,128]{1,0:T(8,128)(2,1)} %dr.1, bf16[512,128]{1,0:T(8,128)(2,1)} %dc.1), custom_call_target="tpu_custom_call" | custom-call | flops 4294967296 | bytes 16777216 | tf_op jit(solution)/shard_map/pallas_call | solution.py:347
  162.4 2.3 %copy.30 = f32[512,512]{1,0:T(8,128)} copy(f32[512,512]{1,0:T(8,128)} %get-tuple-element.4) | data formatting | bytes 2097152
  164.7 2.3 %copy.31 = f32[512,512]{1,0:T(8,128)} copy(f32[512,512]{1,0:T(8,128)} %get-tuple-element.5) | data formatting | bytes 2097152
  (8 shorter events, 0.1 us)

commit v3 on v2

v3 whole, which is shorter than its diff:
```python
import functools

import jax
import jax.numpy as jnp
from jax import lax
from jax.experimental import pallas as pl
from jax.experimental.pallas import tpu as pltpu
from jax.sharding import PartitionSpec as P

RING = 4
CORES = 2
W = 128
CHUNKS = tuple((g, off, 64) for g in range(4) for off in (0, 64))
F32, BF16 = jnp.float32, jnp.bfloat16


def kernel(nz, tiles, slots, keys, mask, t_hbm, c_hbm, dr, dc, out_r, out_c, *scratch):
    n = len(CHUNKS)
    groups = c_hbm.shape[1] // (nz * W)
    it = iter(scratch)
    take = lambda k: [next(it) for _ in range(k)]
    raw, sa, ra, sb, rb, us = (take(n) for _ in range(6))
    uz = take(groups)
    amat = take(groups)
    tv, own, total, tbl_v, tbl = take(5)
    (a_sem, tv_sem, loc_sem, e1_send, sib_send, e1_recv, fw_send, ea_send, ea_recv, eb_send, eb_recv,
     es_send, es_recv, z_send, z_recv, tbl_sem) = take(16)

    z, t = lax.axis_index("aux"), lax.axis_index("tile")
    c, x, y = t % CORES, (t // CORES) % RING, t // (CORES * RING)

    def tid(yy, xx, cc):
        return (yy * RING + xx) * CORES + cc

    def pick(for0, for1):
        return for0 + c * (for1 - for0)

    def first(d):
        return pick(tid(y, (x + RING + d) % RING, 0), tid((y + RING + d) % RING, x, 1))

    def second(d):
        return pick(tid((y + RING + d) % RING, x, 0), tid(y, (x + RING + d) % RING, 1))

    sibling = tid(y, x, 1 - c)
    m1, m2 = pick(x, y), pick(y, x)
    g_opp, g_p, g_m = (m2 + 2) % RING, (m2 + 1) % RING, (m2 + 3) % RING
    z_to = ((z + 1) % nz, (z + nz - 1) % nz)
    sent = []

    def remote(src, dst, send, recv, zz, tt):
        return pltpu.make_async_remote_copy(
            src_ref=src, dst_ref=dst, send_sem=send, recv_sem=recv,
            device_id=(zz, tt), device_id_type=pl.DeviceIdType.MESH)

    def go(src, dst, send, recv, zz, tt):
        copy = remote(src, dst, send, recv, zz, tt)
        copy.start()
        sent.append(copy)

    def arrived(ref, recv):
        remote(ref, ref, a_sem.at[0], recv, z, sibling).wait_recv()

    def rows_of(i, h):
        g, off, rows = CHUNKS[i]
        return pl.ds(pl.multiple_of(g * W + off + h * (rows // 2), 16), rows // 2)

    def slot(i, s):
        return raw[i].at[s, pl.ds(0, tiles)]

    head = CHUNKS[0][2]
    spans = (pl.ds(0, head), pl.ds(head, tv.shape[1] - head))

    def load_tiles(k):
        def body(e, carry):
            pltpu.make_async_copy(
                t_hbm.at[spans[k], pl.ds(pl.multiple_of(e * W, W), W)],
                tv.at[e, spans[k]], tv_sem.at[k]).start()
            return carry

        lax.fori_loop(0, tiles, body, 0)

    def loaded(k):
        span = tv.at[:, spans[k]]
        pltpu.make_async_copy(span, span, tv_sem.at[k]).wait()

    a_copies = []

    def load_coupling():
        for g in range(groups):
            for b in range(nz):
                copy = pltpu.make_async_copy(
                    c_hbm.at[:, pl.ds((b * groups + g) * W, W)],
                    amat[g].at[:, pl.ds(b * W, W)], a_sem.at[g])
                copy.start()
                a_copies.append(copy)

    def empty_tiles(i):
        for s in range(2 * RING):
            raw[i][s, tiles] = jnp.zeros(raw[i].shape[2:], BF16)

    def build_table():
        half = 2 * RING * slots
        row = lax.broadcasted_iota(jnp.int32, (half, 1), 0)
        gg, co, sl = row // (CORES * slots), row // slots % CORES, row % slots
        want = pick((gg * RING + x) * CORES + co, (y * RING + gg) * CORES + co) * slots + sl
        lane = lax.broadcasted_iota(jnp.int32, (half, keys.shape[1]), 1)
        entry = lax.broadcasted_iota(jnp.int32, (half, W), 1)
        for side in range(2):
            hit = keys[side:side + 1, :] == want
            table = jnp.zeros((half, W), jnp.int32)
            for s in range(2 * RING):
                a = (m1 + s // CORES) % RING
                low = tid(pick(y, a), pick(a, x), s % CORES) * tiles
                here = hit & (lane >= low) & (lane < low + tiles)
                least = jnp.min(jnp.where(here, lane, 1 << 20), axis=1, keepdims=True)
                most = jnp.max(jnp.where(here, lane, -1), axis=1, keepdims=True)
                k0 = jnp.where(most >= 0, least - low, tiles)
                k1 = jnp.where(most > least, most - low, tiles)
                table = jnp.where(entry == 2 * s, k0, jnp.where(entry == 2 * s + 1, k1, table))
            tbl_v[side * half:(side + 1) * half, :] = table
        copy = pltpu.make_async_copy(tbl_v, tbl, tbl_sem.at[0])
        copy.start()
        copy.wait()

    barrier = pltpu.get_barrier_semaphore()
    near = [(z, sibling), (z_to[0], t), (z_to[1], t)]
    for d in (1, -1):
        near.append((z, first(d)))
        near.append((z, second(d)))
    for who in near:
        pl.semaphore_signal(barrier, inc=1, device_id=who, device_id_type=pl.DeviceIdType.MESH)
    load_tiles(0)
    empty_tiles(0)
    pl.semaphore_wait(barrier, len(near))

    def local(i):
        return pltpu.make_async_copy(tv.at[:, rows_of(i, c)], slot(i, c), loc_sem.at[i])

    def to_sibling(i):
        go(tv.at[:, rows_of(i, 1 - c)], slot(i, c), sib_send.at[i], e1_recv.at[i, c], z, sibling)
        local(i).start()

    def start_own(i):
        send_raw(i, 0, c, tv.at[:, rows_of(i, c)])

    def start_sib(i):
        arrived(slot(i, 1 - c), e1_recv.at[i, 1 - c])
        send_raw(i, 1, 1 - c, slot(i, 1 - c))

    def send_raw(i, k, cc, src):
        for m, d in enumerate((1, -1)):
            s = ((RING - d) % RING) * CORES + cc
            go(src, slot(i, s), e1_send.at[i, 2 * k + m], e1_recv.at[i, s], z, first(d))

    def start_raw(i):
        start_own(i)
        start_sib(i)

    def forward_raw(i):
        for m, (d, s, cc) in enumerate(((1, 6 + c, c), (-1, 2 + 1 - c, 1 - c))):
            arrived(slot(i, s), e1_recv.at[i, s])
            go(slot(i, s), slot(i, 4 + cc), fw_send.at[i, m], e1_recv.at[i, 4 + cc], z, first(d))

    def finish_raw(i):
        local(i).wait()
        for s in (6 + 1 - c, 2 + c, 4, 5):
            arrived(slot(i, s), e1_recv.at[i, s])

    def summed(i, g, j):
        acc = None
        row = (j // slots % 2) * (2 * RING * slots) + (g * CORES + j // (2 * slots)) * slots + j % slots
        for e in range(4 * RING):
            v = raw[i][e // 2, tbl[row, e]].astype(F32)
            acc = v if acc is None else acc + v
        return acc

    def fill(i, g, low, high, store, extra=None):
        def body(j, carry):
            v = summed(i, g, j)
            if extra is not None:
                v = v + extra[j - low].astype(F32)
            store[j] = v.astype(store.dtype)
            return carry

        lax.fori_loop(low, high, body, 0)

    def scatter_a(i):
        fill(i, g_opp, 0, 16, sa[i])
        go(sa[i].at[pl.ds(0, 8)], ra[i].at[0], ea_send.at[i, 0], ea_recv.at[i, 0], z, second(1))
        go(sa[i].at[pl.ds(8, 8)], ra[i].at[1], ea_send.at[i, 1], ea_recv.at[i, 1], z, second(-1))

    def scatter_b(i):
        fill(i, g_p, 8, 16, sb[i].at[0])
        fill(i, g_m, 0, 8, sb[i].at[1])
        arrived(ra[i].at[0], ea_recv.at[i, 0])
        fill(i, g_p, 0, 8, sb[i].at[0], ra[i].at[0])
        go(sb[i].at[0], rb[i].at[0], eb_send.at[i, 0], eb_recv.at[i, 0], z, second(1))
        arrived(ra[i].at[1], ea_recv.at[i, 1])
        fill(i, g_m, 8, 16, sb[i].at[1], ra[i].at[1])
        go(sb[i].at[1], rb[i].at[1], eb_send.at[i, 1], eb_recv.at[i, 1], z, second(-1))
        fill(i, m2, 0, 16, own.at[:, pl.ds(0, CHUNKS[i][2] // 2)])

    def part(i, zz, first_row, rows):
        g, off, _ = CHUNKS[i]
        return uz[g].at[zz, pl.ds(pl.multiple_of(off + first_row, 16), rows)]

    def owners(i):
        g, off, rows = CHUNKS[i]
        half = rows // 2
        mine = pl.ds(pl.multiple_of(off + c * half, 16), half)
        for k in range(2):
            arrived(rb[i].at[k], eb_recv.at[i, k])

        def position(j):
            return own[j, :half] + rb[i][0, j].astype(F32) + rb[i][1, j].astype(F32)

        for jj in range(8):
            us[i][:, jj * W:(jj + 1) * W] = position((1 - c) * 8 + jj).astype(BF16)
        go(us[i], part(i, z, c * half, half), es_send.at[i], es_recv.at[i], z, sibling)
        for jj in range(8):
            uz[g][z, mine, jj * W:(jj + 1) * W] = position(c * 8 + jj).astype(BF16)

    last = nz // 2 - 1

    def z_part(i, k, step, origin):
        rows = CHUNKS[i][2]
        if step == last:
            return part(i, origin, k * (rows // 2), rows // 2)
        return part(i, origin, 0, rows)

    def z_copy(i, k, step):
        ref = z_part(i, k, step, (z + (nz - step if k == 0 else step)) % nz)
        go(ref, ref, z_send.at[i, k, step], z_recv.at[i, k, step], z_to[k], t)

    def z_wait(i, k, step):
        origin = (z + (2 * nz - 1 - step if k == 0 else step + 1)) % nz
        arrived(z_part(i, k, step, origin), z_recv.at[i, k, step])

    def z_begin(i):
        half = CHUNKS[i][2] // 2
        arrived(part(i, z, (1 - c) * half, half), es_recv.at[i])
        for k in range(2):
            z_copy(i, k, 0)

    def z_forward(i, step):
        for k in range(2):
            z_wait(i, k, step - 1)
            z_copy(i, k, step)

    def z_end(i):
        for k in range(2):
            z_wait(i, k, last)

    def masked():
        for copy in a_copies:
            copy.wait()
        rows = amat[0].shape[0] // W
        for g in range(groups):
            def body(e, carry):
                b, p = e // rows, e % rows
                keep = mask[z * rows + p, b * groups + g].astype(F32)
                at = (pl.ds(pl.multiple_of(p * W, W), W), pl.ds(pl.multiple_of(b * W, W), W))
                amat[g][at] = (amat[g][at].astype(F32) * keep).astype(BF16)
                return carry

            lax.fori_loop(0, nz * rows, body, 0)

    step_n = 256

    def product(g):
        def body(e, carry):
            at = pl.ds(pl.multiple_of(e * step_n, step_n), step_n)
            right = uz[g][:, :, at].reshape(nz * W, step_n)
            new = jnp.dot(amat[g][...], right, preferred_element_type=F32)
            if g > 0:
                new = new + total[:, at]
            total[:, at] = new
            return carry

        lax.fori_loop(0, total.shape[1] // step_n, body, 0)

    def done_group(i):
        g, off, rows = CHUNKS[i]
        return g if off + rows == W else None

    def ring_end(i):
        z_end(i)
        if done_group(i) is not None:
            product(done_group(i))

    def ring_end(i):
        z_end(i)
        if done_group(i) is not None:
            product(done_group(i))

    loaded(0)
    to_sibling(0)
    start_own(0)
    load_tiles(1)
    start_sib(0)
    load_coupling()
    build_table()
    loaded(1)
    for i in range(1, n):
        to_sibling(i)
    forward_raw(0)
    for i in range(1, min(n, 3)):
        start_raw(i)
    for i in range(1, n):
        empty_tiles(i)
    for k in range(-2, n + 2):
        if k > -2:
            if k + 3 < n:
                forward_raw(k + 3)
            if k + 5 < n:
                start_raw(k + 5)
        if k + 2 < n:
            finish_raw(k + 2)
            scatter_a(k + 2)
        if k == -2:
            if n > 1:
                forward_raw(1)
            if n > 3:
                start_raw(3)
        if 0 <= k + 1 < n:
            owners(k + 1)
        if 0 <= k - 2 < n:
            ring_end(k - 2)
        if 0 <= k + 1 < n:
            z_begin(k + 1)
        if 0 <= k < n:
            z_forward(k, 2)
        if k + 2 < n:
            scatter_b(k + 2)
        if k == -1:
            masked()
        if 0 <= k + 1 < n:
            z_forward(k + 1, 1)
        if 0 <= k < n:
            z_forward(k, 3)

    blocks = dr.shape[0] // W
    for k, (dens, out) in enumerate(((dr, out_r), (dc, out_c))):
        for b in range(blocks):
            at = (k * blocks + b) * W
            s = total[:, at:at + W]
            high = s.astype(BF16)
            low = (s - high.astype(F32)).astype(BF16)
            d = dens[b * W:(b + 1) * W, :]
            out[:, b * W:(b + 1) * W] = jnp.dot(high, d, preferred_element_type=F32) + jnp.dot(
                low, d, preferred_element_type=F32)
    for copy in sent:
        copy.wait_send()


def shards(transformed, coupling, block_mask, density_row, density_col,
           row_owner, row_slot, col_owner, col_slot):
    nz = lax.axis_size("aux")
    aux_dev, pairs = transformed.shape
    tiles = pairs // W
    slots = density_row.shape[0] // W
    columns = 2 * density_row.shape[0]
    groups = aux_dev // W
    keys = jnp.stack([(row_owner * slots + row_slot)[:, 0], (col_owner * slots + col_slot)[:, 0]])
    keys = jnp.pad(keys, ((0, 0), (0, -keys.shape[1] % W)), constant_values=-1)
    n = len(CHUNKS)
    halves = [c[2] // 2 for c in CHUNKS]
    scratch = []
    scratch += [pltpu.VMEM((2 * RING, tiles + 1, h, W), BF16) for h in halves]
    scratch += [pltpu.VMEM((16, h, W), BF16) for h in halves]
    scratch += [pltpu.VMEM((2, 8, h, W), BF16) for h in halves]
    scratch += [pltpu.VMEM((2, 16, h, W), BF16) for h in halves]
    scratch += [pltpu.VMEM((2, 16, h, W), BF16) for h in halves]
    scratch += [pltpu.VMEM((h, columns), BF16) for h in halves]
    scratch += [pltpu.VMEM((nz, W, columns), BF16) for _ in range(groups)]
    scratch += [pltpu.VMEM((aux_dev, nz * W), BF16) for _ in range(groups)]
    scratch += [pltpu.VMEM((tiles, aux_dev, W), BF16)]
    scratch += [pltpu.VMEM((16, max(halves), W), F32), pltpu.VMEM((aux_dev, columns), F32),
                pltpu.VMEM((4 * RING * slots, W), jnp.int32),
                pltpu.SMEM((4 * RING * slots, W), jnp.int32)]
    dma = pltpu.SemaphoreType.DMA
    steps = nz // 2
    scratch += [dma((groups,)), dma((2,)), dma((n,)), dma((n, 4)), dma((n,)), dma((n, 8)), dma((n, 2)),
                dma((n, 2)), dma((n, 2)), dma((n, 2)), dma((n, 2)), dma((n,)), dma((n,)),
                dma((n, 2, steps)), dma((n, 2, steps)), dma((1,))]
    vmem, smem = pl.BlockSpec(memory_space=pltpu.VMEM), pl.BlockSpec(memory_space=pltpu.SMEM)
    hbm = pl.BlockSpec(memory_space=pl.ANY)
    shape = jax.ShapeDtypeStruct((aux_dev, columns // 2), F32)
    return pl.pallas_call(
        functools.partial(kernel, nz, tiles, slots),
        out_shape=(shape, shape),
        in_specs=[vmem, smem, hbm, hbm, vmem, vmem],
        out_specs=(vmem, vmem),
        scratch_shapes=scratch,
        compiler_params=pltpu.CompilerParams(
            collective_id=0, has_side_effects=True, vmem_limit_bytes=56 * 1024 * 1024),
        cost_estimate=pl.CostEstimate(
            flops=2 * aux_dev * nz * aux_dev * columns, bytes_accessed=16 << 20,
            transcendentals=0),
    )(keys, block_mask, transformed, coupling, density_row, density_col)


def solution(mesh):
    placed = (P("aux", "tile"), P("aux", None), P(), P("tile", None), P("tile", None),
              P(), P(), P(), P())
    return jax.shard_map(shards, mesh=mesh, in_specs=placed,
                         out_specs=(P("aux", "tile"), P("aux", "tile")), check_vma=False)
```

time: 168 us -> 142 us (0.85)
  Pallas kernels: 151 us -> 135 us
  other arithmetic: 8.35 us -> 0.76 us
    pallas_call x1, Pallas kernels: 151 us -> 135 us  [shards(): pl.pallas_call(functools.partial(kernel, nz, tiles, slots), out_shape=(sh...]
    reduce_min x1 -> x0, other arithmetic: 4.6 us -> none  [tables(): spot = jnp.min(jnp.where(hit, k, tiles), axis=-1)]
    reduce_sum x1 -> x0, other arithmetic: 1.96 us -> none  [tables(): rank = jnp.sum(earlier.astype(jnp.int32), axis=-1)]
    unnamed x3 -> x2, local copies, waits for them, and re-layouts: 4.53 us -> 4.52 us
where the time goes in v3:
time: 142 us; the launch traced here: 141 us
  Pallas kernels  135 us (95%)
  local copies, waits for them, and re-layouts  5.13 us (4%)
    pallas_call x1, Pallas kernels, shards(): pl.pallas_call(functools.partial(kernel, nz, tiles, slots), out_shape=(sh...  135 us
    unnamed x2, local copies, waits for them, and re-layouts  4.52 us

profile of v3, /device:TPU:2, one launch (start us, length us, event | category | flops | bytes accessed | tf_op | source)
XLA Modules:
  0.0 141.3 jit_solution(13384746856151988164)
XLA Ops:
  0.6 0.7 add_bitcast_fusion
  1.4 0.6 pad.4.keys
  2.0 134.8 %shard_map.104 = (f32[512,512]{1,0:T(8,128)}, f32[512,512]{1,0:T(8,128)}) custom-call(s32[2,896]{1,0:T(2,128)} %pad.4.keys, s32[32,32]{1,0:T(8,128)} %mask.1, bf16[512,3328]{1,0:T(8,128)(2,1)} %t_hbm.1, bf16[512,4096]{1,0:T(8,128)(2,1)} %c_hbm.1, bf16[512,128]{1,0:T(8,128)(2,1)} %dr.1, bf16[512,128]{1,0:T(8,128)(2,1)} %dc.1), custom_call_target="tpu_custom_call" | custom-call | flops 4294967296 | bytes 16777216 | tf_op jit(solution)/shard_map/pallas_call | solution.py:389
  136.8 2.3 %copy.13 = f32[512,512]{1,0:T(8,128)} copy(f32[512,512]{1,0:T(8,128)} %get-tuple-element.6) | data formatting | bytes 2097152
  139.1 2.3 %copy.14 = f32[512,512]{1,0:T(8,128)} copy(f32[512,512]{1,0:T(8,128)} %get-tuple-element.7) | data formatting | bytes 2097152
  (1 shorter events, 0.0 us)

commit v4 on v3

--- a/solution.py
+++ b/solution.py
@@ -10,21 +10,21 @@
 RING = 4
 CORES = 2
 W = 128
-CHUNKS = tuple((g, off, 64) for g in range(4) for off in (0, 64))
+CHUNKS = ((0, 0, 32), (0, 32, 32), (0, 64, 64)) + tuple((g, off, 64) for g in (1, 2, 3) for off in (0, 64))
 F32, BF16 = jnp.float32, jnp.bfloat16
 
 
-def kernel(nz, tiles, slots, keys, mask, t_hbm, c_hbm, dr, dc, out_r, out_c, *scratch):
+def kernel(nz, tiles, slots, keys, mask, t_hbm, c_hbm, total, *scratch):
     n = len(CHUNKS)
     groups = c_hbm.shape[1] // (nz * W)
     it = iter(scratch)
     take = lambda k: [next(it) for _ in range(k)]
-    raw, sa, ra, sb, rb, us = (take(n) for _ in range(6))
+    raw, pb, rp, sa, ra, sb, rb, us = (take(n) for _ in range(8))
     uz = take(groups)
     amat = take(groups)
-    tv, own, total, tbl_v, tbl = take(5)
-    (a_sem, tv_sem, loc_sem, e1_send, sib_send, e1_recv, fw_send, ea_send, ea_recv, eb_send, eb_recv,
-     es_send, es_recv, z_send, z_recv, tbl_sem) = take(16)
+    tv, own, tbl_v, tbl = take(4)
+    (a_sem, tv_sem, loc_sem, e1_send, sib_send, e1_recv, pb_send, pb_recv, ea_send, ea_recv, eb_send, eb_recv,
+     es_send, es_recv, z_send, z_recv, tbl_sem) = take(17)
 
     z, t = lax.axis_index("aux"), lax.axis_index("tile")
     c, x, y = t % CORES, (t // CORES) % RING, t // (CORES * RING)
@@ -35,15 +35,17 @@
     def pick(for0, for1):
         return for0 + c * (for1 - for0)
 
-    def first(d):
-        return pick(tid(y, (x + RING + d) % RING, 0), tid((y + RING + d) % RING, x, 1))
+    def first(at):
+        return pick(tid(y, at, 0), tid(at, x, 1))
 
     def second(d):
         return pick(tid((y + RING + d) % RING, x, 0), tid(y, (x + RING + d) % RING, 1))
 
     sibling = tid(y, x, 1 - c)
     m1, m2 = pick(x, y), pick(y, x)
+    pair, across = m1 + 1 - 2 * (m1 % 2), RING - 1 - m1
     g_opp, g_p, g_m = (m2 + 2) % RING, (m2 + 1) % RING, (m2 + 3) % RING
+    order = (g_opp, g_p, g_m, m2)
     z_to = ((z + 1) % nz, (z + nz - 1) % nz)
     sent = []
 
@@ -95,21 +97,22 @@
                 a_copies.append(copy)
 
     def empty_tiles(i):
-        for s in range(2 * RING):
+        for s in range(2 * CORES):
             raw[i][s, tiles] = jnp.zeros(raw[i].shape[2:], BF16)
 
     def build_table():
         half = 2 * RING * slots
         row = lax.broadcasted_iota(jnp.int32, (half, 1), 0)
         gg, co, sl = row // (CORES * slots), row // slots % CORES, row % slots
-        want = pick((gg * RING + x) * CORES + co, (y * RING + gg) * CORES + co) * slots + sl
         lane = lax.broadcasted_iota(jnp.int32, (half, keys.shape[1]), 1)
         entry = lax.broadcasted_iota(jnp.int32, (half, W), 1)
-        for side in range(2):
+        for block in range(4):
+            at, side = (m1, across)[block // 2], block % 2
+            want = pick((gg * RING + at) * CORES + co, (at * RING + gg) * CORES + co) * slots + sl
             hit = keys[side:side + 1, :] == want
             table = jnp.zeros((half, W), jnp.int32)
-            for s in range(2 * RING):
-                a = (m1 + s // CORES) % RING
+            for s in range(2 * CORES):
+                a = (m1, pair)[s // CORES]
                 low = tid(pick(y, a), pick(a, x), s % CORES) * tiles
                 here = hit & (lane >= low) & (lane < low + tiles)
                 least = jnp.min(jnp.where(here, lane, 1 << 20), axis=1, keepdims=True)
@@ -117,20 +120,22 @@
                 k0 = jnp.where(most >= 0, least - low, tiles)
                 k1 = jnp.where(most > least, most - low, tiles)
                 table = jnp.where(entry == 2 * s, k0, jnp.where(entry == 2 * s + 1, k1, table))
-            tbl_v[side * half:(side + 1) * half, :] = table
+            tbl_v[block * half:(block + 1) * half, :] = table
         copy = pltpu.make_async_copy(tbl_v, tbl, tbl_sem.at[0])
         copy.start()
         copy.wait()
 
     barrier = pltpu.get_barrier_semaphore()
     near = [(z, sibling), (z_to[0], t), (z_to[1], t)]
-    for d in (1, -1):
-        near.append((z, first(d)))
-        near.append((z, second(d)))
+    near += [(z, first(pair)), (z, first(across)), (z, second(1)), (z, second(-1))]
     for who in near:
         pl.semaphore_signal(barrier, inc=1, device_id=who, device_id_type=pl.DeviceIdType.MESH)
     load_tiles(0)
-    empty_tiles(0)
+    build_table()
+    load_tiles(1)
+    for i in range(n):
+        empty_tiles(i)
+    loaded(0)
     pl.semaphore_wait(barrier, len(near))
 
     def local(i):
@@ -148,57 +153,64 @@
         send_raw(i, 1, 1 - c, slot(i, 1 - c))
 
     def send_raw(i, k, cc, src):
-        for m, d in enumerate((1, -1)):
-            s = ((RING - d) % RING) * CORES + cc
-            go(src, slot(i, s), e1_send.at[i, 2 * k + m], e1_recv.at[i, s], z, first(d))
+        to = CORES + cc
+        go(src, slot(i, to), e1_send.at[i, k], e1_recv.at[i, to], z, first(pair))
 
     def start_raw(i):
         start_own(i)
         start_sib(i)
 
-    def forward_raw(i):
-        for m, (d, s, cc) in enumerate(((1, 6 + c, c), (-1, 2 + 1 - c, 1 - c))):
-            arrived(slot(i, s), e1_recv.at[i, s])
-            go(slot(i, s), slot(i, 4 + cc), fw_send.at[i, m], e1_recv.at[i, 4 + cc], z, first(d))
-
     def finish_raw(i):
         local(i).wait()
-        for s in (6 + 1 - c, 2 + c, 4, 5):
+        for s in (2, 3):
             arrived(slot(i, s), e1_recv.at[i, s])
 
-    def summed(i, g, j):
+    def scatter_pair(i):
+        for k, (low, high) in enumerate(((0, 1), (1, RING))):
+            for r in range(low, high):
+                fill(i, 1, order[r], 0, 16, pb[i].at[r])
+            span = pl.ds(low, high - low)
+            go(pb[i].at[span], rp[i].at[span], pb_send.at[i, k], pb_recv.at[i, k], z, first(across))
+
+    def arrived_pair(i, k):
+        arrived(rp[i].at[pl.ds(0, 1) if k == 0 else pl.ds(1, RING - 1)], pb_recv.at[i, k])
+
+    def summed(i, w, g, j):
         acc = None
-        row = (j // slots % 2) * (2 * RING * slots) + (g * CORES + j // (2 * slots)) * slots + j % slots
-        for e in range(4 * RING):
+        row = ((w * 2 + j // slots % 2) * (2 * RING * slots)
+               + (g * CORES + j // (2 * slots)) * slots + j % slots)
+        for e in range(4 * CORES):
             v = raw[i][e // 2, tbl[row, e]].astype(F32)
             acc = v if acc is None else acc + v
         return acc
 
-    def fill(i, g, low, high, store, extra=None):
+    def fill(i, w, g, low, high, store, *extras):
         def body(j, carry):
-            v = summed(i, g, j)
-            if extra is not None:
-                v = v + extra[j - low].astype(F32)
+            v = summed(i, w, g, j)
+            for ref, start in extras:
+                v = v + ref[j - start].astype(F32)
             store[j] = v.astype(store.dtype)
             return carry
 
         lax.fori_loop(low, high, body, 0)
 
     def scatter_a(i):
-        fill(i, g_opp, 0, 16, sa[i])
+        arrived_pair(i, 0)
+        fill(i, 0, g_opp, 0, 16, sa[i], (rp[i].at[0], 0))
         go(sa[i].at[pl.ds(0, 8)], ra[i].at[0], ea_send.at[i, 0], ea_recv.at[i, 0], z, second(1))
         go(sa[i].at[pl.ds(8, 8)], ra[i].at[1], ea_send.at[i, 1], ea_recv.at[i, 1], z, second(-1))
 
     def scatter_b(i):
-        fill(i, g_p, 8, 16, sb[i].at[0])
-        fill(i, g_m, 0, 8, sb[i].at[1])
+        arrived_pair(i, 1)
+        fill(i, 0, g_p, 8, 16, sb[i].at[0], (rp[i].at[1], 0))
+        fill(i, 0, g_m, 0, 8, sb[i].at[1], (rp[i].at[2], 0))
         arrived(ra[i].at[0], ea_recv.at[i, 0])
-        fill(i, g_p, 0, 8, sb[i].at[0], ra[i].at[0])
+        fill(i, 0, g_p, 0, 8, sb[i].at[0], (rp[i].at[1], 0), (ra[i].at[0], 0))
         go(sb[i].at[0], rb[i].at[0], eb_send.at[i, 0], eb_recv.at[i, 0], z, second(1))
         arrived(ra[i].at[1], ea_recv.at[i, 1])
-        fill(i, g_m, 8, 16, sb[i].at[1], ra[i].at[1])
+        fill(i, 0, g_m, 8, 16, sb[i].at[1], (rp[i].at[2], 0), (ra[i].at[1], 8))
         go(sb[i].at[1], rb[i].at[1], eb_send.at[i, 1], eb_recv.at[i, 1], z, second(-1))
-        fill(i, m2, 0, 16, own.at[:, pl.ds(0, CHUNKS[i][2] // 2)])
+        fill(i, 0, m2, 0, 16, own.at[:, pl.ds(0, CHUNKS[i][2] // 2)], (rp[i].at[3], 0))
 
     def part(i, zz, first_row, rows):
         g, off, _ = CHUNKS[i]
@@ -293,52 +305,46 @@
         if done_group(i) is not None:
             product(done_group(i))
 
-    loaded(0)
     to_sibling(0)
     start_own(0)
-    load_tiles(1)
     start_sib(0)
-    load_coupling()
-    build_table()
     loaded(1)
     for i in range(1, n):
         to_sibling(i)
-    forward_raw(0)
-    for i in range(1, min(n, 3)):
+    for i in range(1, min(n, 2)):
         start_raw(i)
-    for i in range(1, n):
-        empty_tiles(i)
-    for k in range(-2, n + 2):
-        if k > -2:
-            if k + 3 < n:
-                forward_raw(k + 3)
-            if k + 5 < n:
-                start_raw(k + 5)
-        if k + 2 < n:
-            finish_raw(k + 2)
-            scatter_a(k + 2)
-        if k == -2:
-            if n > 1:
-                forward_raw(1)
-            if n > 3:
-                start_raw(3)
+    for k in range(-4, n + 2):
         if 0 <= k + 1 < n:
             owners(k + 1)
+        if 0 <= k + 2 < n:
+            scatter_b(k + 2)
+        if 0 <= k < n:
+            z_forward(k, 1)
+        if 0 <= k - 1 < n:
+            z_forward(k - 1, 3)
+        if 0 <= k + 3 < n:
+            scatter_a(k + 3)
+        if k + 6 < n:
+            start_raw(k + 6)
+        if k + 4 < n:
+            finish_raw(k + 4)
+            scatter_pair(k + 4)
+        if k == -3:
+            load_coupling()
+        if k == min(0, n - 2):
+            masked()
         if 0 <= k - 2 < n:
             ring_end(k - 2)
         if 0 <= k + 1 < n:
             z_begin(k + 1)
         if 0 <= k < n:
             z_forward(k, 2)
-        if k + 2 < n:
-            scatter_b(k + 2)
-        if k == -1:
-            masked()
-        if 0 <= k + 1 < n:
-            z_forward(k + 1, 1)
-        if 0 <= k < n:
-            z_forward(k, 3)
-
+
+    for copy in sent:
+        copy.wait_send()
+
+
+def densities(total, dr, dc, out_r, out_c):
     blocks = dr.shape[0] // W
     for k, (dens, out) in enumerate(((dr, out_r), (dc, out_c))):
         for b in range(blocks):
@@ -349,8 +355,6 @@
             d = dens[b * W:(b + 1) * W, :]
             out[:, b * W:(b + 1) * W] = jnp.dot(high, d, preferred_element_type=F32) + jnp.dot(
                 low, d, preferred_element_type=F32)
-    for copy in sent:
-        copy.wait_send()
 
 
 def shards(transformed, coupling, block_mask, density_row, density_col,
@@ -366,7 +370,9 @@
     n = len(CHUNKS)
     halves = [c[2] // 2 for c in CHUNKS]
     scratch = []
-    scratch += [pltpu.VMEM((2 * RING, tiles + 1, h, W), BF16) for h in halves]
+    scratch += [pltpu.VMEM((2 * CORES, tiles + 1, h, W), BF16) for h in halves]
+    scratch += [pltpu.VMEM((RING, 16, h, W), BF16) for h in halves]
+    scratch += [pltpu.VMEM((RING, 16, h, W), BF16) for h in halves]
     scratch += [pltpu.VMEM((16, h, W), BF16) for h in halves]
     scratch += [pltpu.VMEM((2, 8, h, W), BF16) for h in halves]
     scratch += [pltpu.VMEM((2, 16, h, W), BF16) for h in halves]
@@ -375,29 +381,36 @@
     scratch += [pltpu.VMEM((nz, W, columns), BF16) for _ in range(groups)]
     scratch += [pltpu.VMEM((aux_dev, nz * W), BF16) for _ in range(groups)]
     scratch += [pltpu.VMEM((tiles, aux_dev, W), BF16)]
-    scratch += [pltpu.VMEM((16, max(halves), W), F32), pltpu.VMEM((aux_dev, columns), F32),
-                pltpu.VMEM((4 * RING * slots, W), jnp.int32),
-                pltpu.SMEM((4 * RING * slots, W), jnp.int32)]
+    scratch += [pltpu.VMEM((16, max(halves), W), F32),
+                pltpu.VMEM((8 * RING * slots, W), jnp.int32),
+                pltpu.SMEM((8 * RING * slots, W), jnp.int32)]
     dma = pltpu.SemaphoreType.DMA
     steps = nz // 2
-    scratch += [dma((groups,)), dma((2,)), dma((n,)), dma((n, 4)), dma((n,)), dma((n, 8)), dma((n, 2)),
+    scratch += [dma((groups,)), dma((2,)), dma((n,)), dma((n, 2)), dma((n,)), dma((n, 4)), dma((n, 2)), dma((n, 2)),
                 dma((n, 2)), dma((n, 2)), dma((n, 2)), dma((n, 2)), dma((n,)), dma((n,)),
                 dma((n, 2, steps)), dma((n, 2, steps)), dma((1,))]
     vmem, smem = pl.BlockSpec(memory_space=pltpu.VMEM), pl.BlockSpec(memory_space=pltpu.SMEM)
     hbm = pl.BlockSpec(memory_space=pl.ANY)
-    shape = jax.ShapeDtypeStruct((aux_dev, columns // 2), F32)
-    return pl.pallas_call(
+    sums = pl.pallas_call(
         functools.partial(kernel, nz, tiles, slots),
-        out_shape=(shape, shape),
-        in_specs=[vmem, smem, hbm, hbm, vmem, vmem],
-        out_specs=(vmem, vmem),
+        out_shape=jax.ShapeDtypeStruct((aux_dev, columns), F32),
+        in_specs=[vmem, smem, hbm, hbm],
+        out_specs=vmem,
         scratch_shapes=scratch,
         compiler_params=pltpu.CompilerParams(
             collective_id=0, has_side_effects=True, vmem_limit_bytes=56 * 1024 * 1024),
         cost_estimate=pl.CostEstimate(
             flops=2 * aux_dev * nz * aux_dev * columns, bytes_accessed=16 << 20,
             transcendentals=0),
-    )(keys, block_mask, transformed, coupling, density_row, density_col)
+    )(keys, block_mask, transformed, coupling)
+    shape = jax.ShapeDtypeStruct((aux_dev, columns // 2), F32)
+    whole = pl.BlockSpec(density_row.shape, lambda i: (0, 0))
+    out = pl.BlockSpec((W, columns // 2), lambda i: (i, 0))
+    return pl.pallas_call(
+        densities, out_shape=(shape, shape), grid=(groups,),
+        in_specs=[pl.BlockSpec((W, columns), lambda i: (i, 0)), whole, whole],
+        out_specs=(out, out),
+    )(sums, density_row, density_col)
 
 
 def solution(mesh):

time: 142 us -> 140 us (0.986)
  local copies, waits for them, and re-layouts: 5.13 us -> 0.6 us
  Pallas kernels: 135 us -> 138 us
    unnamed x2 -> x0, local copies, waits for them, and re-layouts: 4.52 us -> none
    pallas_call x1 -> x2, Pallas kernels: 135 us -> 138 us  [the longest x1 133 us: shards(): pl.pallas_call(functools.partial(kernel, nz, tiles, slots), out_shape=jax...]
where the time goes in v4:
time: 140 us
  Pallas kernels  138 us (99%)
    pallas_call x1, Pallas kernels, shards(): pl.pallas_call(functools.partial(kernel, nz, tiles, slots), out_shape=jax...  133 us
    pallas_call x1, Pallas kernels, shards(): pl.pallas_call(densities, out_shape=(shape, shape), grid=(groups,), in_sp...  4.22 us

profile of v4, /device:TPU:2, one launch (start us, length us, event | category | flops | bytes accessed | tf_op | source)
XLA Modules:
  0.0 139.6 jit_solution(16510588306368198915)
XLA Ops:
  0.6 0.7 add_bitcast_fusion
  1.4 0.6 pad.4.keys
  2.0 133.4 %shard_map.104.total = f32[512,1024]{1,0:T(8,128)} custom-call(s32[2,896]{1,0:T(2,128)} %pad.4.keys, s32[32,32]{1,0:T(8,128)} %mask.1, bf16[512,3328]{1,0:T(8,128)(2,1)} %t_hbm.1, bf16[512,4096]{1,0:T(8,128)(2,1)} %c_hbm.1), custom_call_target="tpu_custom_call" | custom-call | flops 4294967296 | bytes 16777216 | tf_op jit(solution)/shard_map/pallas_call | solution.py:394
  135.4 4.2 %shard_map.105 = (f32[512,512]{1,0:T(8,128)}, f32[512,512]{1,0:T(8,128)}) custom-call(f32[512,1024]{1,0:T(8,128)} %shard_map.104.total, bf16[512,128]{1,0:T(8,128)(2,1)} %dr.1, bf16[512,128]{1,0:T(8,128)(2,1)} %dc.1), custom_call_target="tpu_custom_call" | custom-call | tf_op jit(solution)/shard_map/pallas_call | solution.py:409
  (1 shorter events, 0.0 us)

commit v5 on v3

--- a/solution.py
+++ b/solution.py
@@ -14,7 +14,7 @@
 F32, BF16 = jnp.float32, jnp.bfloat16
 
 
-def kernel(nz, tiles, slots, keys, mask, t_hbm, c_hbm, dr, dc, out_r, out_c, *scratch):
+def kernel(nz, tiles, slots, keys, mask, t_hbm, c_hbm, total, *scratch):
     n = len(CHUNKS)
     groups = c_hbm.shape[1] // (nz * W)
     it = iter(scratch)
@@ -22,7 +22,7 @@
     raw, sa, ra, sb, rb, us = (take(n) for _ in range(6))
     uz = take(groups)
     amat = take(groups)
-    tv, own, total, tbl_v, tbl = take(5)
+    tv, own, tbl_v, tbl = take(4)
     (a_sem, tv_sem, loc_sem, e1_send, sib_send, e1_recv, fw_send, ea_send, ea_recv, eb_send, eb_recv,
      es_send, es_recv, z_send, z_recv, tbl_sem) = take(16)
 
@@ -339,6 +339,11 @@
         if 0 <= k < n:
             z_forward(k, 3)
 
+    for copy in sent:
+        copy.wait_send()
+
+
+def densities(total, dr, dc, out_r, out_c):
     blocks = dr.shape[0] // W
     for k, (dens, out) in enumerate(((dr, out_r), (dc, out_c))):
         for b in range(blocks):
@@ -349,8 +354,6 @@
             d = dens[b * W:(b + 1) * W, :]
             out[:, b * W:(b + 1) * W] = jnp.dot(high, d, preferred_element_type=F32) + jnp.dot(
                 low, d, preferred_element_type=F32)
-    for copy in sent:
-        copy.wait_send()
 
 
 def shards(transformed, coupling, block_mask, density_row, density_col,
@@ -375,7 +378,7 @@
     scratch += [pltpu.VMEM((nz, W, columns), BF16) for _ in range(groups)]
     scratch += [pltpu.VMEM((aux_dev, nz * W), BF16) for _ in range(groups)]
     scratch += [pltpu.VMEM((tiles, aux_dev, W), BF16)]
-    scratch += [pltpu.VMEM((16, max(halves), W), F32), pltpu.VMEM((aux_dev, columns), F32),
+    scratch += [pltpu.VMEM((16, max(halves), W), F32),
                 pltpu.VMEM((4 * RING * slots, W), jnp.int32),
                 pltpu.SMEM((4 * RING * slots, W), jnp.int32)]
     dma = pltpu.SemaphoreType.DMA
@@ -385,19 +388,26 @@
                 dma((n, 2, steps)), dma((n, 2, steps)), dma((1,))]
     vmem, smem = pl.BlockSpec(memory_space=pltpu.VMEM), pl.BlockSpec(memory_space=pltpu.SMEM)
     hbm = pl.BlockSpec(memory_space=pl.ANY)
-    shape = jax.ShapeDtypeStruct((aux_dev, columns // 2), F32)
-    return pl.pallas_call(
+    sums = pl.pallas_call(
         functools.partial(kernel, nz, tiles, slots),
-        out_shape=(shape, shape),
-        in_specs=[vmem, smem, hbm, hbm, vmem, vmem],
-        out_specs=(vmem, vmem),
+        out_shape=jax.ShapeDtypeStruct((aux_dev, columns), F32),
+        in_specs=[vmem, smem, hbm, hbm],
+        out_specs=vmem,
         scratch_shapes=scratch,
         compiler_params=pltpu.CompilerParams(
             collective_id=0, has_side_effects=True, vmem_limit_bytes=56 * 1024 * 1024),
         cost_estimate=pl.CostEstimate(
             flops=2 * aux_dev * nz * aux_dev * columns, bytes_accessed=16 << 20,
             transcendentals=0),
-    )(keys, block_mask, transformed, coupling, density_row, density_col)
+    )(keys, block_mask, transformed, coupling)
+    shape = jax.ShapeDtypeStruct((aux_dev, columns // 2), F32)
+    whole = pl.BlockSpec(density_row.shape, lambda i: (0, 0))
+    out = pl.BlockSpec((W, columns // 2), lambda i: (i, 0))
+    return pl.pallas_call(
+        densities, out_shape=(shape, shape), grid=(groups,),
+        in_specs=[pl.BlockSpec((W, columns), lambda i: (i, 0)), whole, whole],
+        out_specs=(out, out),
+    )(sums, density_row, density_col)
 
 
 def solution(mesh):

time: 142 us -> 141 us (level)
  local copies, waits for them, and re-layouts: 5.13 us -> 0.6 us
  Pallas kernels: 135 us -> 138 us
    unnamed x2 -> x0, local copies, waits for them, and re-layouts: 4.52 us -> none
    pallas_call x1 -> x2, Pallas kernels: 135 us -> 138 us  [the longest x1 134 us: shards(): pl.pallas_call(functools.partial(kernel, nz, tiles, slots), out_shape=jax...]
where the time goes in v5:
time: 141 us; the launch traced here: 140 us
  Pallas kernels  138 us (98%)
    pallas_call x1, Pallas kernels, shards(): pl.pallas_call(functools.partial(kernel, nz, tiles, slots), out_shape=jax...  134 us
    pallas_call x1, Pallas kernels, shards(): pl.pallas_call(densities, out_shape=(shape, shape), grid=(groups,), in_sp...  4.22 us

profile of v5, /device:TPU:2, one launch (start us, length us, event | category | flops | bytes accessed | tf_op | source)
XLA Modules:
  0.0 140.4 jit_solution(1639836339275215138)
XLA Ops:
  0.6 0.7 add_bitcast_fusion
  1.4 0.6 pad.4.keys
  2.0 134.1 %shard_map.104.total = f32[512,1024]{1,0:T(8,128)} custom-call(s32[2,896]{1,0:T(2,128)} %pad.4.keys, s32[32,32]{1,0:T(8,128)} %mask.1, bf16[512,3328]{1,0:T(8,128)(2,1)} %t_hbm.1, bf16[512,4096]{1,0:T(8,128)(2,1)} %c_hbm.1), custom_call_target="tpu_custom_call" | custom-call | flops 4294967296 | bytes 16777216 | tf_op jit(solution)/shard_map/pallas_call | solution.py:391
  136.1 4.2 %shard_map.105 = (f32[512,512]{1,0:T(8,128)}, f32[512,512]{1,0:T(8,128)}) custom-call(f32[512,1024]{1,0:T(8,128)} %shard_map.104.total, bf16[512,128]{1,0:T(8,128)(2,1)} %dr.1, bf16[512,128]{1,0:T(8,128)(2,1)} %dc.1), custom_call_target="tpu_custom_call" | custom-call | tf_op jit(solution)/shard_map/pallas_call | solution.py:406
  (1 shorter events, 0.0 us)
